TPU v7x, 32 devices: a whole 2x2x4 slice. The times are simulated.
32 devices in a mesh: seq: 4 (over y, x), tok: 8 (over z, core).
Axes of the slice: x: 2, y: 2, z: 4, core: 2. Of those that a mesh axis runs over, the one named last changes fastest.
Arguments:
- hidden_in: bfloat16 [32, 1024, 768], P('seq', 'tok'), may hold values from -6 to 6
- out_grad: bfloat16 [32, 1024, 768], P('seq', 'tok'), may hold values from -6 to 6
- lengths: int32 [32], P('seq'), may hold values from 20 to 1024, as said below
- w_zx: float32 [768, 3072], P('seq', 'tok')
- m_zx: float32 [768, 3072], P('seq', 'tok'), may hold values from -40 to 40
- v_zx: float32 [768, 3072], P('seq', 'tok'), may hold values from 4 to 16
- w_bc: float32 [768, 304], P('seq', 'tok')
- m_bc: float32 [768, 304], P('seq', 'tok'), may hold values from -40 to 40
- v_bc: float32 [768, 304], P('seq', 'tok'), may hold values from 4 to 16
- w_out: float32 [1536, 768], P('seq', 'tok')
- m_out: float32 [1536, 768], P('seq', 'tok'), may hold values from -40 to 40
- v_out: float32 [1536, 768], P('seq', 'tok'), may hold values from 4 to 16
- conv_w: float32 [4, 1792], replicated, may hold values from -3 to 3
- m_conv: float32 [4, 1792], replicated, may hold values from -64 to 64
- v_conv: float32 [4, 1792], replicated, may hold values from 8 to 32
- vectors: float32 [4216], replicated
- m_vec: float32 [4216], replicated, may hold values from -64 to 64
- v_vec: float32 [4216], replicated, may hold values from 8 to 32
Outputs:
- hidden_out: bfloat16 [32, 1024, 768], P('seq', 'tok')
- hidden_grad: bfloat16 [32, 1024, 768], P('seq', 'tok')
- m_zx_new: float32 [768, 3072], P('seq', 'tok')
- v_zx_new: float32 [768, 3072], P('seq', 'tok')
- w_zx_new: float32 [768, 3072], P('seq', 'tok')
- m_bc_new: float32 [768, 304], P('seq', 'tok')
- v_bc_new: float32 [768, 304], P('seq', 'tok')
- w_bc_new: float32 [768, 304], P('seq', 'tok')
- m_out_new: float32 [1536, 768], P('seq', 'tok')
- v_out_new: float32 [1536, 768], P('seq', 'tok')
- w_out_new: float32 [1536, 768], P('seq', 'tok')
- m_conv_new: float32 [4, 1792], replicated
- v_conv_new: float32 [4, 1792], replicated
- conv_w_new: float32 [4, 1792], replicated
- m_vec_new: float32 [4216], replicated
- v_vec_new: float32 [4216], replicated
- vectors_new: float32 [4216], replicated
- norms: float32 [2, 8], replicated
Inputs may be any that keep to these rules, and one draw needn't show every extreme that they name: `lengths`: each aligned group of 8 sequences holds at least one of length 1024.
All inputs are finite; a program needn't handle non-finite values.
Results may differ from a plain program's by a relative error of at most 0.0044.
The roundings to bfloat16 on the way count: a program that leaves them out, or rounds other values in their place, can miss the bound.
Values may be sent and summed in bfloat16 or wider, within the bound.
No kernel may reach another device: no remote copies, remote signals or barrier semaphores. Data moves between devices by JAX's collectives and lax.ppermute only.
A program may use at most 256 MiB of HBM per device.

v0:
```python
import jax
import jax.numpy as jnp
from jax import lax
from jax.sharding import PartitionSpec as P

D = 768
E = 1536
H = 24
P_SIZE = 64
N = 64
Q = 128
K = 4
L = 1024
STEP = 10


NORM_EPS = 1e-05
UPDATE_EPS = 1e-06
ADAM_EPS = 1e-06
FIRST_DECAY = 0.9
SECOND_DECAY = 0.999
WEIGHT_DECAY = 0.01
LEARN_RATE = 0.3
HIGHEST = lax.Precision.HIGHEST


def shifted(value, axis, steps):
    count = lax.axis_size(axis)
    initial, last = (max(0, -steps), min(count, count - steps))
    return lax.ppermute(value, axis, [(source, source + steps) for source in range(initial, last)])


def rms_scale(values, gain):
    return values * lax.rsqrt(jnp.mean(values * values, -1, keepdims=True) + NORM_EPS) * gain


def gate_scale(values, gate_in, gain):
    gated = values * jax.nn.silu(gate_in)
    return gated * lax.rsqrt(jnp.mean(gated * gated, -1, keepdims=True) + NORM_EPS) * gain


def run_conv(padded, kernel, offset_vec):
    span_rows = padded.shape[1] - (K - 1)
    summed = offset_vec + kernel[0] * padded[:, 0:span_rows]
    for offset in range(1, K):
        summed = summed + kernel[offset] * padded[:, offset : offset + span_rows]
    return jax.nn.silu(summed)


def stretch_scan(inputs, rates, in_map, out_map, backward):
    groups, length, head_count, head_width = inputs.shape
    blocks = length // Q

    def split_blocks(tensor):
        shaped = tensor.reshape((groups, blocks, Q) + tensor.shape[2:])
        return jnp.moveaxis(shaped, 1, 0)

    positions = jnp.arange(Q)
    if backward:
        strict_side = (positions[:, None] < positions[None, :])[None, :, :, None]
    else:
        strict_side = (positions[:, None] > positions[None, :])[None, :, :, None]
    initial = jnp.zeros((groups, head_count, head_width, in_map.shape[-1]), jnp.float32)

    def advance(carry_state, pieces):
        block_in, block_rate, block_enter, block_leave = pieces
        if backward:
            running = lax.cumsum(block_rate, axis=1, reverse=True)
            edge_sum = running[:, 0, :]
        else:
            running = jnp.cumsum(block_rate, axis=1)
            edge_sum = running[:, -1, :]
        before = running - block_rate
        spread = before[:, :, None, :] - running[:, None, :, :]
        decays = jnp.exp(jnp.where(strict_side, spread, -1e30))
        scores = jnp.einsum("gin,gjn->gij", block_leave, block_enter, precision=HIGHEST)
        weights = scores[..., None] * decays
        within = jnp.einsum("gijh,gjhp->gihp", weights, block_in, precision=HIGHEST)
        carried = (
            jnp.einsum("gin,ghpn->gihp", block_leave, carry_state, precision=HIGHEST)
            * jnp.exp(before)[..., None]
        )
        to_edge = jnp.exp(edge_sum[:, None, :] - running)
        state_new = carry_state * jnp.exp(edge_sum)[:, :, None, None] + jnp.einsum(
            "gjhp,gjn->ghpn", block_in * to_edge[..., None], block_enter, precision=HIGHEST
        )
        return (state_new, within + carried)

    pieces = (
        split_blocks(inputs),
        split_blocks(rates),
        split_blocks(in_map),
        split_blocks(out_map),
    )
    _, outputs = lax.scan(jax.checkpoint(advance), initial, pieces, reverse=backward)
    return jnp.moveaxis(outputs, 0, 1).reshape(groups, length, head_count, head_width)


def mixer(conv_out, delta_raw, ssm_params, keep_mask):
    heads = delta_raw.shape[-1] // 2
    width = heads * P_SIZE
    delta_bias = ssm_params[: 2 * heads]
    decay_log = ssm_params[2 * heads : 4 * heads]
    skip_gain = ssm_params[4 * heads :]
    delta = jax.nn.softplus(delta_raw + delta_bias) * keep_mask[..., None]
    rates = -delta * jnp.exp(decay_log)
    groups, length = (conv_out.shape[0], conv_out.shape[1])
    values = conv_out[..., :width].reshape(groups, length, heads, P_SIZE)
    in_fwd = conv_out[..., width : width + N]
    out_fwd = conv_out[..., width + N : width + 2 * N]
    in_back = conv_out[..., width + 2 * N : width + 3 * N]
    out_back = conv_out[..., width + 3 * N :]
    forward_part = stretch_scan(
        values * delta[..., :heads, None], rates[..., :heads], in_fwd, out_fwd, False
    )
    reverse_part = stretch_scan(
        values * delta[..., heads:, None], rates[..., heads:], in_back, out_back, True
    )
    mixed = forward_part + reverse_part + skip_gain[:, None] * values
    return mixed.reshape(groups, length, width)


def adam_step(param, grad, first, second):
    first_new = FIRST_DECAY * first + (1.0 - FIRST_DECAY) * grad
    second_new = SECOND_DECAY * second + (1.0 - SECOND_DECAY) * grad * grad
    corrected = first_new / (1.0 - FIRST_DECAY**STEP)
    scaled = jnp.sqrt(second_new / (1.0 - SECOND_DECAY**STEP))
    return (first_new, second_new, corrected / (scaled + ADAM_EPS) + WEIGHT_DECAY * param)


def segment_norms(param, direction):
    edges = (0, D, D + E, D + 2 * E + 4 * N, param.shape[0])
    weight_sq = jnp.stack(
        [
            jnp.sum(param[edges[index] : edges[index + 1]] * param[edges[index] : edges[index + 1]])
            for index in range(4)
        ]
    )
    update_sq = jnp.stack(
        [
            jnp.sum(
                direction[edges[index] : edges[index + 1]]
                * direction[edges[index] : edges[index + 1]]
            )
            for index in range(4)
        ]
    )
    ratios = jnp.sqrt(weight_sq) / jnp.sqrt(update_sq + UPDATE_EPS)
    spread = jnp.concatenate(
        [
            jnp.zeros((edges[index + 1] - edges[index],), param.dtype) + ratios[index]
            for index in range(4)
        ]
    )
    return (weight_sq, update_sq, spread)


def per_device(
    hidden_in,
    out_grad,
    lengths,
    w_zx,
    m_zx,
    v_zx,
    w_bc,
    m_bc,
    v_bc,
    w_out,
    m_out,
    v_out,
    conv_w,
    m_conv,
    v_conv,
    vectors,
    m_vec,
    v_vec,
):
    tok_count = lax.axis_size("tok")
    seq_group, local_len, _ = hidden_in.shape
    split = tok_count // seq_group
    heads_here = H // split
    width_here = heads_here * P_SIZE
    column_parts = (
        lax.all_gather(w_zx.astype(jnp.bfloat16), "tok", axis=1, tiled=True),
        lax.all_gather(w_bc.astype(jnp.bfloat16), "tok", axis=1, tiled=True),
        lax.all_gather(w_out.astype(jnp.bfloat16), "tok", axis=1, tiled=True),
    )
    proj_zx, proj_bc, proj_out = (
        lax.all_gather(column_parts[0], "seq", axis=0, tiled=True),
        lax.all_gather(column_parts[1], "seq", axis=0, tiled=True),
        lax.all_gather(column_parts[2], "seq", axis=0, tiled=True),
    )
    gain_in = vectors[:D]
    gain_out = vectors[D : D + E]
    conv_bias = vectors[D + E : D + 2 * E + 4 * N]
    ssm_params = vectors[D + 2 * E + 4 * N :]
    tok_index = lax.axis_index("tok")
    seq_slot = tok_index // split
    head_part = tok_index % split
    positions = tok_index * local_len + jnp.arange(local_len)
    token_mask = (positions[None, :] < lengths[:, None]).astype(jnp.float32)
    own_length = lax.dynamic_index_in_dim(lengths, seq_slot, 0, keepdims=False)
    sequence_mask = (jnp.arange(L)[None, :] < own_length).astype(jnp.float32)
    ssm_local = jnp.concatenate(
        [
            lax.dynamic_slice_in_dim(ssm_params, piece * H + head_part * heads_here, heads_here)
            for piece in range(5)
        ]
    )
    hidden = hidden_in.astype(jnp.float32)
    normed, norm_pull = jax.vjp(rms_scale, hidden, gain_in)
    normed_low = normed.astype(jnp.bfloat16)
    zx_out = jnp.einsum("gtd,de->gte", normed_low, proj_zx, preferred_element_type=jnp.float32)
    bc_out = jnp.einsum("gtd,de->gte", normed_low, proj_bc, preferred_element_type=jnp.float32)
    gate_in = zx_out[..., :E]
    pre_conv = jnp.concatenate([zx_out[..., E:], bc_out[..., : 4 * N]], -1).astype(jnp.bfloat16)
    delta_raw = bc_out[..., 4 * N :].astype(jnp.bfloat16)
    rim_rows = shifted(pre_conv[:, local_len - (K - 1) :, :], "tok", 1)
    padded = jnp.concatenate([rim_rows, pre_conv], 1).astype(jnp.float32)
    conv_vals, conv_pull = jax.vjp(run_conv, padded, conv_w, conv_bias)
    conv_low = conv_vals.astype(jnp.bfloat16)
    value_part = conv_low[..., :E].reshape(seq_group, local_len, split, width_here)
    map_part = conv_low[:, :, None, E:]
    value_map = jnp.concatenate([value_part, map_part], -1).transpose(0, 2, 1, 3)
    value_map = value_map.reshape(seq_group * split, local_len, width_here + 4 * N)
    delta_part = delta_raw.reshape(seq_group, local_len, 2, split, heads_here).transpose(
        0, 3, 1, 2, 4
    )
    delta_part = delta_part.reshape(seq_group * split, local_len, 2 * heads_here)
    seq_conv, delta_seq = (
        lax.all_to_all(value_map, "tok", split_axis=0, concat_axis=1, tiled=True),
        lax.all_to_all(delta_part, "tok", split_axis=0, concat_axis=1, tiled=True),
    )

    def mix_local(conv_vals_in, delta_vals, params):
        return mixer(conv_vals_in, delta_vals, params, sequence_mask)

    mixed, mix_pull = jax.vjp(
        mix_local, seq_conv.astype(jnp.float32), delta_seq.astype(jnp.float32), ssm_local
    )
    came_back = lax.all_to_all(
        mixed.astype(jnp.bfloat16), "tok", split_axis=1, concat_axis=0, tiled=True
    )
    returned = (
        came_back.reshape(seq_group, split, local_len, width_here)
        .transpose(0, 2, 1, 3)
        .reshape(seq_group, local_len, E)
    )
    gated_norm, gate_pull = jax.vjp(gate_scale, returned.astype(jnp.float32), gate_in, gain_out)
    gated_low = gated_norm.astype(jnp.bfloat16)
    branch = jnp.einsum("gte,ed->gtd", gated_low, proj_out, preferred_element_type=jnp.float32)
    hidden_out = (hidden + token_mask[..., None] * branch).astype(jnp.bfloat16)
    upstream = out_grad.astype(jnp.float32)
    branch_grad = (upstream * token_mask[..., None]).astype(jnp.bfloat16)
    grad_out_w = jnp.einsum(
        "gte,gtd->ed", gated_low, branch_grad, preferred_element_type=jnp.float32
    )
    gated_grad = jnp.einsum(
        "gtd,ed->gte", branch_grad, proj_out, preferred_element_type=jnp.float32
    )
    mixed_grad, gate_grad, gain_out_grad = gate_pull(gated_grad)
    grad_payload = (
        mixed_grad.astype(jnp.bfloat16)
        .reshape(seq_group, local_len, split, width_here)
        .transpose(0, 2, 1, 3)
    )
    grad_payload = grad_payload.reshape(seq_group * split, local_len, width_here)
    mixed_back = lax.all_to_all(grad_payload, "tok", split_axis=0, concat_axis=1, tiled=True)
    conv_grad_seq, delta_grad, ssm_grad_local = mix_pull(mixed_back.astype(jnp.float32))
    came_conv, came_delta = (
        lax.all_to_all(conv_grad_seq, "tok", split_axis=1, concat_axis=0, tiled=True),
        lax.all_to_all(delta_grad, "tok", split_axis=1, concat_axis=0, tiled=True),
    )
    came_conv = came_conv.reshape(seq_group, split, local_len, width_here + 4 * N)
    value_back = came_conv[..., :width_here].transpose(0, 2, 1, 3).reshape(seq_group, local_len, E)
    map_back = jnp.sum(came_conv[..., width_here:], axis=1)
    delta_back = came_delta.reshape(seq_group, split, local_len, 2, heads_here).transpose(
        0, 2, 3, 1, 4
    )
    delta_back = delta_back.reshape(seq_group, local_len, 2 * H).astype(jnp.bfloat16)
    conv_grad_low = jnp.concatenate([value_back, map_back], -1).astype(jnp.bfloat16)
    padded_grad, kernel_grad, bias_grad = conv_pull(conv_grad_low.astype(jnp.float32))
    edge_rows = shifted(padded_grad[:, : K - 1, :].astype(jnp.bfloat16), "tok", -1).astype(
        jnp.float32
    )
    inner_grad = padded_grad[:, K - 1 :, :]
    pre_grad = jnp.concatenate(
        [
            inner_grad[:, : local_len - (K - 1), :],
            inner_grad[:, local_len - (K - 1) :, :] + edge_rows,
        ],
        1,
    ).astype(jnp.bfloat16)
    zx_grad = jnp.concatenate([gate_grad.astype(jnp.bfloat16), pre_grad[..., :E]], -1)
    bc_grad = jnp.concatenate([pre_grad[..., E:], delta_back], -1)
    grad_zx_w = jnp.einsum("gtd,gte->de", normed_low, zx_grad, preferred_element_type=jnp.float32)
    grad_bc_w = jnp.einsum("gtd,gte->de", normed_low, bc_grad, preferred_element_type=jnp.float32)
    normed_grad = jnp.einsum("gte,de->gtd", zx_grad, proj_zx, preferred_element_type=jnp.float32)
    normed_grad = normed_grad + jnp.einsum(
        "gte,de->gtd", bc_grad, proj_bc, preferred_element_type=jnp.float32
    )
    hidden_part, gain_in_grad = norm_pull(normed_grad)
    hidden_grad = (upstream + hidden_part).astype(jnp.bfloat16)
    summed_cols = (
        lax.psum_scatter(grad_zx_w, "tok", scatter_dimension=1, tiled=True),
        lax.psum_scatter(grad_bc_w, "tok", scatter_dimension=1, tiled=True),
        lax.psum_scatter(grad_out_w, "tok", scatter_dimension=1, tiled=True),
    )
    zx_sum, bc_sum, out_sum = (
        lax.psum_scatter(summed_cols[0], "seq", scatter_dimension=0, tiled=True),
        lax.psum_scatter(summed_cols[1], "seq", scatter_dimension=0, tiled=True),
        lax.psum_scatter(summed_cols[2], "seq", scatter_dimension=0, tiled=True),
    )
    ssm_grad = jnp.zeros((5 * H,), jnp.float32)
    for piece in range(5):
        ssm_grad = lax.dynamic_update_slice_in_dim(
            ssm_grad,
            ssm_grad_local[piece * heads_here : (piece + 1) * heads_here],
            piece * H + head_part * heads_here,
            0,
        )
    vec_grad = jnp.concatenate([gain_in_grad, gain_out_grad, bias_grad, ssm_grad])
    kernel_sum, vec_sum = lax.psum((kernel_grad, vec_grad), ("seq", "tok"))
    zx_first, zx_second, zx_dir = adam_step(w_zx, zx_sum, m_zx, v_zx)
    bc_first, bc_second, bc_dir = adam_step(w_bc, bc_sum, m_bc, v_bc)
    out_first, out_second, out_dir = adam_step(w_out, out_sum, m_out, v_out)
    weight_sq = jnp.stack([jnp.sum(w_zx * w_zx), jnp.sum(w_bc * w_bc), jnp.sum(w_out * w_out)])
    update_sq = jnp.stack(
        [jnp.sum(zx_dir * zx_dir), jnp.sum(bc_dir * bc_dir), jnp.sum(out_dir * out_dir)]
    )
    weight_all, update_all = lax.psum((weight_sq, update_sq), ("seq", "tok"))
    ratios = jnp.sqrt(weight_all) / jnp.sqrt(update_all + UPDATE_EPS)
    zx_new = w_zx - LEARN_RATE * ratios[0] * zx_dir
    bc_new = w_bc - LEARN_RATE * ratios[1] * bc_dir
    out_new = w_out - LEARN_RATE * ratios[2] * out_dir
    conv_first, conv_second, conv_dir = adam_step(conv_w, kernel_sum, m_conv, v_conv)
    conv_wsq = jnp.sum(conv_w * conv_w)
    conv_usq = jnp.sum(conv_dir * conv_dir)
    conv_new = (
        conv_w - LEARN_RATE * (jnp.sqrt(conv_wsq) / jnp.sqrt(conv_usq + UPDATE_EPS)) * conv_dir
    )
    vec_first, vec_second, vec_dir = adam_step(vectors, vec_sum, m_vec, v_vec)
    seg_weight, seg_update, seg_ratio = segment_norms(vectors, vec_dir)
    vectors_new = vectors - LEARN_RATE * seg_ratio * vec_dir
    norms = jnp.stack(
        [
            jnp.sqrt(jnp.concatenate([weight_all, conv_wsq[None], seg_weight])),
            jnp.sqrt(jnp.concatenate([update_all, conv_usq[None], seg_update])),
        ]
    )
    return (
        hidden_out,
        hidden_grad,
        zx_first,
        zx_second,
        zx_new,
        bc_first,
        bc_second,
        bc_new,
        out_first,
        out_second,
        out_new,
        conv_first,
        conv_second,
        conv_new,
        vec_first,
        vec_second,
        vectors_new,
        norms,
    )


def solution(mesh):
    placed = (
        P("seq", "tok", None),
        P("seq", "tok", None),
        P("seq"),
        P("seq", "tok"),
        P("seq", "tok"),
        P("seq", "tok"),
        P("seq", "tok"),
        P("seq", "tok"),
        P("seq", "tok"),
        P("seq", "tok"),
        P("seq", "tok"),
        P("seq", "tok"),
        P(),
        P(),
        P(),
        P(),
        P(),
        P(),
    )
    return jax.shard_map(
        per_device,
        mesh=mesh,
        in_specs=placed,
        out_specs=(
            P("seq", "tok", None),
            P("seq", "tok", None),
            P("seq", "tok"),
            P("seq", "tok"),
            P("seq", "tok"),
            P("seq", "tok"),
            P("seq", "tok"),
            P("seq", "tok"),
            P("seq", "tok"),
            P("seq", "tok"),
            P("seq", "tok"),
            P(),
            P(),
            P(),
            P(),
            P(),
            P(),
            P(),
        ),
        check_vma=False,
    )
```

profile of v0, /device:TPU:0, one launch (start us, length us, event | category | flops | bytes accessed | tf_op | source)
XLA Modules:
  0.0 2642.7 jit_solution(12024425605118786524)
XLA Ops:
  9.1 26.9 %all-gather.5.cloned.1.call-done = bf16[192,3072]{1,0:T(8,128)(2,1)} async-done(((bf16[192,384]{1,0:T(8,128)(2,1)}), bf16[192,3072]{1,0:T(8,128)(2,1)}) %all-gather.5.cloned.1.call-update) | async-done | bytes 1179664 | tf_op jit(solution)/shard_map/all_gather | solution.py:184
  77.9 21.3 all-gather.7.cloned.1.call-done
  132.4 78.2 %all-to-all-done.1 = bf16[8,128,1792]{2,1,0:T(8,128)(2,1)} async-done(((bf16[8,128,1792]{2,1,0:T(8,128)(2,1)}), bf16[8,128,1792]{2,1,0:T(8,128)(2,1)}, u32[]{:S(2)}, u32[]{:S(2)}) %all-to-all-start.1) | async-done | bytes 3670048 | tf_op jit(solution)/shard_map/all_to_all | solution.py:231
  253.9 258.9 %while.79 = (s32[]{:T(128)}, f32[1,24,64,64]{3,2,1,0:T(8,128)S(1)}, f32[8,1,128,24,64]{2,0,1,4,3:T(8,128)}, f32[8,1,24,64,64]{4,3,2,1,0:T(8,128)}, f32[8,1,128,2...) while((s32[]{:T(128)}, f32[1,24,64,64]{3,2,1,0:T(8,128)S(1)}, ...), condition=%wide.region_6.7_spmd.clone, body=%wide.region_4.6_spmd.clone.sunk | while | flops 619219968 | bytes 8355052 | solution.py:95
  294.5 20.8 dynamic_update_slice.140
  359.1 20.8 dynamic_update_slice.140
  456.1 20.8 dynamic_update_slice.140
  488.5 20.8 dynamic_update_slice.140
  528.2 258.5 %while.78 = (s32[]{:T(128)}, f32[1,24,64,64]{3,2,1,0:T(8,128)S(1)}, f32[8,1,128,24,64]{2,0,1,4,3:T(8,128)}, f32[8,1,24,64,64]{4,3,2,1,0:T(8,128)}, f32[8,1,128,2...) while((s32[]{:T(128)}, f32[1,24,64,64]{3,2,1,0:T(8,128)S(1)}, ...), condition=%wide.region_3.4_spmd.clone, body=%wide.region_1.3_spmd.clone.sunk | while | flops 619219968 | bytes 8356045 | solution.py:95
  536.5 20.8 dynamic_update_slice.138
  568.7 20.8 dynamic_update_slice.138
  601.0 20.8 dynamic_update_slice.138
  633.3 20.8 dynamic_update_slice.138
  665.7 20.8 dynamic_update_slice.138
  698.0 20.8 dynamic_update_slice.138
  730.3 20.8 dynamic_update_slice.138
  762.6 20.8 dynamic_update_slice.138
  816.9 35.4 %copy.781 = bf16[1,1024,1536]{2,0,1:T(2,128)(2,1)} copy(bf16[1,1024,1536]{2,1,0:T(8,128)(2,1)S(1)} %add_convert_fusion) | data formatting | bytes 6291456 | tf_op jit(solution)/shard_map/convert_element_type | solution.py:242
  881.5 80.8 %all_gather.22 = bf16[384,768]{0,1:T(8,128)(2,1)} all-gather(bf16[384,96]{0,1:T(8,128)(2,1)S(1)} %convert_element_type.177), channel_id=1, replica_groups=mesh['seq'=4,'tok'=8] {'tok'}, dimensions={1}, use_global_device_ids=true | all-gather | bytes 663552 | tf_op jit(solution)/shard_map/all_gather | solution.py:186
  979.1 22.6 all-gather.9.cloned.1.call-done
  1044.3 51.5 %all-to-all-done.3 = bf16[8,128,1536]{2,1,0:T(8,128)(2,1)S(1)} async-done(((bf16[8,128,1536]{2,1,0:T(8,128)(2,1)}), bf16[8,128,1536]{2,1,0:T(8,128)(2,1)S(1)}, u32[]{:S(2)}, u32[]{:S(2)}) %all-to-all-start.3) | async-done | bytes 3145760 | tf_op jit(solution)/shard_map/all_to_all | solution.py:268
  1105.4 460.5 %while.80 = (s32[]{:T(128)}, f32[1,24,64,64]{3,2,1,0:T(8,128)}, f32[8,1,128,24,64]{2,0,1,4,3:T(8,128)}, f32[8,1,128,24]{3,2,1,0:T(8,128)}, f32[8,1,128,64]{2,0,1...) while((s32[]{:T(128)}, f32[1,24,64,64]{3,2,1,0:T(8,128)}, ...), condition=%wide.region_19.20_spmd.clone, body=%wide.region_9.19_spmd.clone.sunk | while | flops 1404525568 | bytes 21100680 | solution.py:95
  1197.5 20.8 dynamic_update_slice.142
  1370.4 20.8 dynamic_update_slice.142
  1571.6 466.6 %while.81 = (s32[]{:T(128)}, f32[1,24,64,64]{3,2,1,0:T(8,128)}, f32[8,1,128,24,64]{2,0,1,4,3:T(8,128)}, f32[8,1,128,24]{3,2,1,0:T(8,128)}, f32[8,1,128,64]{2,0,1...) while((s32[]{:T(128)}, f32[1,24,64,64]{3,2,1,0:T(8,128)}, ...), condition=%wide.region_30.31_spmd.clone, body=%wide.region_20.30_spmd.clone.sunk | while | flops 1404525568 | bytes 20313704 | solution.py:95
  2096.1 52.2 %copy.780 = bf16[1,1024,1792]{2,0,1:T(2,128)(2,1)} copy(bf16[1,1024,1792]{2,1,0:T(8,128)(2,1)S(1)} %pad_add_fusion.1) | data formatting | bytes 7340032 | tf_op jit(solution)/shard_map/transpose(jvp())/add_any | solution.py:108
  2148.3 38.7 %reduce.75 = bf16[1024,1792]{1,0:T(8,128)(2,1)} reduce(bf16[1024,1,1792]{2,1,0:T(2,128)(2,1)} %bitcast.892, bf16[]{:T(256)} %broadcast.958), dimensions={1}, to_apply=%bitcast.613.reduce_sub_computation | reduce | bytes 7340034
  2204.8 114.7 %all-to-all-done.4 = bf16[8,2,114688]{2,1,0:T(2,128)(2,1)} async-done(((bf16[8,2,114688]{2,1,0:T(2,128)(2,1)}), bf16[8,2,114688]{2,1,0:T(2,128)(2,1)}, u32[]{:S(2)}, u32[]{:S(2)}) %all-to-all-start.4) | async-done | bytes 3670048 | tf_op jit(solution)/shard_map/all_to_all | solution.py:271
  2429.1 29.9 %fusion.8 = f32[768,40]{0,1:T(8,128)S(1)} fusion(f32[768,304]{0,1:T(8,128)} %convolution_bitcast_fusion.16), kind=kCustom, calls=%all-reduce-scatter | all-reduce-scatter fusion | flops 245761 | bytes 1057280
  2464.3 38.9 %reduce-scatter.10.cloned.1.call-done = f32[768,384]{1,0:T(8,128)} async-done(((f32[768,3072]{1,0:T(8,128)}), f32[768,384]{1,0:T(8,128)}) %reduce-scatter.10.cloned.1.call-update) | async-done | bytes 1179664 | tf_op jit(solution)/shard_map/reduce_scatter | solution.py:305
  2531.3 30.1 %reduce-scatter.12.cloned.1.call-done = f32[192,384]{1,0:T(8,128)} async-done(((f32[768,384]{1,0:T(8,128)}), f32[192,384]{1,0:T(8,128)}) %reduce-scatter.12.cloned.1.call-update) | async-done | bytes 294928 | tf_op jit(solution)/shard_map/reduce_scatter | solution.py:310
  2567.2 40.1 %all-reduce.24 = (f32[3]{0:T(128)S(1)}, f32[3]{0:T(128)S(1)}, f32[4,1792]{1,0:T(4,128)S(1)}, f32[4216]{0:T(1024)S(1)}) all-reduce(f32[3]{0:T(128)S(1)} %get-tuple-element.1354, f32[3]{0:T(128)S(1)} %get-tuple-element.1353, f32[4,1792]{1,0:T(4,128)S(1)} %pad_add_fusion.3, ...), channel_id=1, replica_groups=mesh['seq'=4,'tok'=8] {'seq','tok'}, use_global_device_ids=true, to_apply=%region_47.48 | all-reduce | flops 11390 | bytes 91120 | tf_op jit(solution)/shard_map/psum | solution.py:331
  (1304 shorter events, 1667.0 us)
Async XLA Ops:
  7.2 92.0 %copy-start.7 = (bf16[8,128,768]{2,1,0:T(8,128)(2,1)S(1)}, bf16[8,128,768]{2,1,0:T(8,128)(2,1)}, u32[]{:S(2)}) copy-start(bf16[8,128,768]{2,1,0:T(8,128)(2,1)} %param.26) | copy-start | bytes 4718596
  7.2 70.0 %copy-start.48 = (f32[4216]{0:T(1024)S(1)}, f32[4216]{0:T(1024)}, u32[]{:S(2)}) copy-start(f32[4216]{0:T(1024)} %param.41) | copy-start | bytes 50596
  7.2 28.7 %all-gather.5.cloned.1.call-start = ((), (), s32[]{:S(2)}) async-start(), calls=%async_computation.11 | async-start | bytes 1327104 | tf_op jit(solution)/shard_map/all_gather | solution.py:184
  9.0 90.1 %all-gather.7.cloned.1.call-start = ((), (), s32[]{:S(2)}) async-start(), calls=%async_computation.12 | async-start | bytes 5898240 | tf_op jit(solution)/shard_map/all_gather | solution.py:189
  72.3 47.4 %all-to-all-start = ((bf16[8,128,48]{1,2,0:T(8,128)(2,1)}), bf16[8,128,48]{1,2,0:T(8,128)(2,1)S(1)}, u32[]{:S(2)}, u32[]{:S(2)}) async-start(bf16[8,128,48]{1,2,0:T(8,128)(2,1)} %slice.274), calls=%async_computation | async-start | bytes 196608 | tf_op jit(solution)/shard_map/all_to_all | solution.py:232
  106.7 2.7 collective-permute-start
  119.7 90.8 %all-to-all-start.1 = ((bf16[8,128,1792]{2,1,0:T(8,128)(2,1)}), bf16[8,128,1792]{2,1,0:T(8,128)(2,1)}, u32[]{:S(2)}, u32[]{:S(2)}) async-start(bf16[8,128,1792]{2,1,0:T(8,128)(2,1)} %maximum_bitcast_fusion), calls=%async_computation.1 | async-start | bytes 7340032 | tf_op jit(solution)/shard_map/all_to_all | solution.py:231
  128.0 682.8 %copy-start.52 = (f32[1536]{0:T(1024)}, f32[1536]{0:T(1024)S(1)}, u32[]{:S(2)}) copy-start(f32[1536]{0:T(1024)S(1)} %mul.1197) | copy-start | bytes 18436
  130.0 83.1 %copy-start.23 = (f32[1,1024,48]{1,2,0:T(8,128)}, f32[1,1024,48]{1,2,0:T(8,128)S(1)}, u32[]{:S(2)}) copy-start(f32[1,1024,48]{1,2,0:T(8,128)S(1)} %reshape.2098) | copy-start | bytes 589828
  877.8 87.5 %all-to-all-start.2 = ((bf16[8,2,98304]{2,1,0:T(2,128)(2,1)}), bf16[8,2,98304]{2,1,0:T(2,128)(2,1)S(1)}, u32[]{:S(2)}, u32[]{:S(2)}) async-start(bf16[8,2,98304]{2,1,0:T(2,128)(2,1)} %reshape.2159), calls=%async_computation.2 | async-start | bytes 6291456 | tf_op jit(solution)/shard_map/all_to_all | solution.py:241
  881.4 120.3 %all-gather.9.cloned.1.call-start = ((), (), s32[]{:S(2)}) async-start(), calls=%async_computation.13 | async-start | bytes 2949120 | tf_op jit(solution)/shard_map/all_gather | solution.py:191
  1019.6 76.3 %all-to-all-start.3 = ((bf16[8,128,1536]{2,1,0:T(8,128)(2,1)}), bf16[8,128,1536]{2,1,0:T(8,128)(2,1)S(1)}, u32[]{:S(2)}, u32[]{:S(2)}) async-start(bf16[8,128,1536]{2,1,0:T(8,128)(2,1)} %get-tuple-element.1314), calls=%async_computation.3 | async-start | bytes 6291456 | tf_op jit(solution)/shard_map/all_to_all | solution.py:268
  2193.7 125.8 %all-to-all-start.4 = ((bf16[8,2,114688]{2,1,0:T(2,128)(2,1)}), bf16[8,2,114688]{2,1,0:T(2,128)(2,1)}, u32[]{:S(2)}, u32[]{:S(2)}) async-start(bf16[8,2,114688]{2,1,0:T(2,128)(2,1)} %reshape.2161), calls=%async_computation.4 | async-start | bytes 7340032 | tf_op jit(solution)/shard_map/all_to_all | solution.py:271
  2198.2 166.6 %reduce-scatter.14.cloned.1.call-start = ((), (), s32[]{:S(2)}) async-start(), calls=%async_computation.16 | async-start | bytes 5308416 | tf_op jit(solution)/shard_map/reduce_scatter | solution.py:307
  2204.7 257.7 %reduce-scatter.16.cloned.1.call-start = ((), (), s32[]{:S(2)}) async-start(), calls=%async_computation.17 | async-start | bytes 737280 | tf_op jit(solution)/shard_map/reduce_scatter | solution.py:312
  2363.5 4.6 collective-permute-start.1
  2364.9 138.4 %reduce-scatter.10.cloned.1.call-start = ((), (), s32[]{:S(2)}) async-start(), calls=%async_computation.14 | async-start | bytes 10616832 | tf_op jit(solution)/shard_map/reduce_scatter | solution.py:305
  2411.9 12.9 all-to-all-start.5
  2417.0 112.6 %reduce-scatter.18.cloned.1.call-start = ((), (), s32[]{:S(2)}) async-start(), calls=%async_computation.18 | async-start | bytes 491520
  2426.1 77.2 %copy-start.14 = (bf16[768,304]{1,0:T(8,128)(2,1)S(1)}, bf16[768,304]{1,0:T(8,128)(2,1)}, u32[]{:S(2)}) copy-start(bf16[768,304]{1,0:T(8,128)(2,1)} %copy-done.13) | copy-start | bytes 1400836
  2459.0 2.2 collective-permute-start.2
  2462.3 99.0 %reduce-scatter.12.cloned.1.call-start = ((), (), s32[]{:S(2)}) async-start(), calls=%async_computation.15 | async-start | bytes 1474560 | tf_op jit(solution)/shard_map/reduce_scatter | solution.py:310
  2464.2 165.9 %copy-start.37 = (f32[384,96]{0,1:T(8,128)}, f32[384,96]{0,1:T(8,128)S(1)}, u32[]{:S(2)}) copy-start(f32[384,96]{0,1:T(8,128)S(1)} %get-tuple-element.1287) | copy-start | bytes 442372
  2464.2 165.9 %copy-start.38 = (f32[384,96]{0,1:T(8,128)}, f32[384,96]{0,1:T(8,128)S(1)}, u32[]{:S(2)}) copy-start(f32[384,96]{0,1:T(8,128)S(1)} %get-tuple-element.1288) | copy-start | bytes 442372
  2513.8 47.6 %copy-start.12 = (f32[192,384]{1,0:T(8,128)S(1)}, f32[192,384]{1,0:T(8,128)}, u32[]{:S(2)}) copy-start(f32[192,384]{1,0:T(8,128)} %param.29) | copy-start | bytes 884740
  2513.8 93.5 %copy-start.68 = (f32[4216]{0:T(1024)S(1)}, f32[4216]{0:T(1024)}, u32[]{:S(2)}) copy-start(f32[4216]{0:T(1024)} %param.43) | copy-start | bytes 50596
  2513.8 93.5 %copy-start.69 = (f32[4216]{0:T(1024)S(1)}, f32[4216]{0:T(1024)}, u32[]{:S(2)}) copy-start(f32[4216]{0:T(1024)} %param.42) | copy-start | bytes 50596
  2513.8 96.5 %copy-start.47 = (f32[4,1792]{1,0:T(4,128)S(1)}, f32[4,1792]{1,0:T(4,128)}, u32[]{:S(2)}) copy-start(f32[4,1792]{1,0:T(4,128)} %param.38) | copy-start | bytes 86020
  2531.3 104.3 %copy-start.50 = (f32[192,38]{0,1:T(8,128)}, f32[192,38]{0,1:T(8,128)S(1)}, u32[]{:S(2)}) copy-start(f32[192,38]{0,1:T(8,128)S(1)} %get-tuple-element.1285) | copy-start | bytes 87556
  2531.3 104.3 %copy-start.51 = (f32[192,38]{0,1:T(8,128)}, f32[192,38]{0,1:T(8,128)S(1)}, u32[]{:S(2)}) copy-start(f32[192,38]{0,1:T(8,128)S(1)} %get-tuple-element.1286) | copy-start | bytes 87556
  2563.3 72.3 %copy-start.34 = (f32[192,384]{1,0:T(8,128)}, f32[192,384]{1,0:T(8,128)S(1)}, u32[]{:S(2)}) copy-start(f32[192,384]{1,0:T(8,128)S(1)} %get-tuple-element.1283) | copy-start | bytes 884740
  2563.3 72.3 %copy-start.35 = (f32[192,384]{1,0:T(8,128)}, f32[192,384]{1,0:T(8,128)S(1)}, u32[]{:S(2)}) copy-start(f32[192,384]{1,0:T(8,128)S(1)} %get-tuple-element.1284) | copy-start | bytes 884740
  (134 other events, 1391.0 us)
Sparse Core Ops, SparseCore 0:
  10.2 25.6 all-gather.4
  37.8 61.3 all-gather.6
  964.6 37.0 all-gather.8
  2204.9 111.5 reduce-scatter.13
  2365.0 25.6 reduce-scatter.15
  2392.9 110.2 reduce-scatter.9
  2506.2 23.3 reduce-scatter.17
  2532.8 28.5 reduce-scatter.11
where the time goes:
time: 2680 us; the launch traced here: 2640 us
  local copies, waits for them, and re-layouts  1170 us (44%)
  matrix products  478 us (18%)
  waiting for transfers between devices  406 us (15%)
  other arithmetic  347 us (13%)
  blocking collectives  180 us (7%)
  starting transfers between devices  35.2 us (1%)
    dynamic_update_slice x64, local copies, waits for them, and re-layouts, stretch_scan(): lax.scan(jax.checkpoint(advance), initial, pieces, reverse=backward)  721 us
    dot_general x48, matrix products, advance(): within = jnp.einsum('gijh,gjhp->gihp', weights, block_in, precision=HIGHEST)  193 us
    all_to_all x1, waiting for transfers between devices, per_device(): lax.all_to_all(conv_grad_seq, 'tok', split_axis=1, concat_axis=0, tiled=T...  115 us
    dot_general x64, matrix products, advance(): jnp.einsum('gin,ghpn->gihp', block_leave, carry_state, precision=HIGHEST)  98.8 us
    dot_general x48, matrix products, advance(): jnp.einsum('gjhp,gjn->ghpn', block_in * to_edge[..., None], block_enter,...  97.7 us
    all_gather x1, blocking collectives, per_device(): lax.all_gather(w_out.astype(jnp.bfloat16), 'tok', axis=1, tiled=True)  80.8 us
    all_to_all x1, waiting for transfers between devices, per_device(): lax.all_to_all(value_map, 'tok', split_axis=0, concat_axis=1, tiled=True)  78.2 us
    unnamed x10, other arithmetic  62.1 us
  transfers between devices with their start and end apart: 17, of which 12 were waited for; matrix products, arithmetic and copies ran while one was open for 8% of the time, Pallas kernels for 0%

commit v1 on v0

v1 whole, which is shorter than its diff:
```python
import numpy as np
import jax
import jax.numpy as jnp
from jax import lax
from jax.experimental import pallas as pl
from jax.experimental.pallas import tpu as pltpu
from jax.sharding import PartitionSpec as P

D = 768
E = 1536
H = 24
P_SIZE = 64
N = 64
Q = 128
K = 4
L = 1024
STEP = 10


NORM_EPS = 1e-05
UPDATE_EPS = 1e-06
ADAM_EPS = 1e-06
FIRST_DECAY = 0.9
SECOND_DECAY = 0.999
WEIGHT_DECAY = 0.01
LEARN_RATE = 0.3
HIGHEST = lax.Precision.HIGHEST


QB = 128
XW = E
MW = 4 * N
CW = XW + MW
PW = CW + 128
PAIRS = H // 2
HALO = 16
CHUNK = 256
F32 = jnp.float32
LOG2_E = 1.4426950408889634
BF16 = jnp.bfloat16
VMEM_BYTES = 58 * 1024 * 1024
GROUP = 256
GROUPS = XW // GROUP
GROUP_HEADS = GROUP // P_SIZE


def dot(a, b):
    return jnp.dot(a, b, preferred_element_type=F32)


def dot_nt(a, b):
    return lax.dot_general(a, b, (((1,), (1,)), ((), ())), preferred_element_type=F32)


def dot_tn(a, b):
    return lax.dot_general(a, b, (((0,), (0,)), ((), ())), preferred_element_type=F32)


def dot_exact(a, b):
    return jnp.dot(a, b, preferred_element_type=F32, precision=HIGHEST)


def iota(shape, dim):
    return lax.broadcasted_iota(jnp.int32, shape, dim)


def sigmoid(value):
    return 0.5 + 0.5 * jnp.tanh(0.5 * value)


def split(value):
    high = value.astype(BF16)
    return high, (value - high.astype(F32)).astype(BF16)


def doubled(value):
    return jnp.concatenate([value, value], 1)


def halves(pair):
    lane = iota(pair.shape, 1)
    zero = jnp.zeros_like(pair)
    return jnp.concatenate(
        [jnp.where(lane < P_SIZE, pair, zero), jnp.where(lane < P_SIZE, zero, pair)], 0
    )


def keep_tile(length, block):
    rows = block * QB + iota((QB, QB), 0)
    return jnp.where((rows < length) & (iota((QB, QB), 1) < 2 * H), 1.0, 0.0).astype(F32)


def edge_row(run):
    return jnp.where(iota((1, QB), 1) < H, run[QB - 1 : QB], run[0:1])


def two_parts(tile):
    return jnp.concatenate(split(tile), 1)


def lanes(group):
    return slice(group * GROUP, (group + 1) * GROUP)


def back_lanes(group):
    return slice(XW + group * GROUP, XW + (group + 1) * GROUP)


def decay_of(before, run_t, delta_t, lower, head):
    back = H + head
    ahead = before[:, head : head + 1] - run_t[head : head + 1]
    behind = before[:, back : back + 1] - run_t[back : back + 1]
    decay = jnp.exp2(jnp.minimum(jnp.minimum(ahead, behind), 0.0))
    step = jnp.where(lower, delta_t[head : head + 1], delta_t[back : back + 1])
    return decay, step


def spread_matrix():
    col = np.arange(2 * XW)[None]
    row = np.arange(2 * QB)[:, None]
    return jnp.asarray(row % QB == H * (col // XW) + col % XW // P_SIZE, BF16)


def block_scores(in_fwd, out_fwd, in_back, out_back):
    row = iota((QB, QB), 0)
    col = iota((QB, QB), 1)
    lower = row > col
    ahead = dot_nt(out_fwd, in_fwd)
    behind = dot_nt(out_back, in_back)
    return lower, jnp.where(lower, ahead, jnp.where(row < col, behind, 0.0))


def conv_pieces(ext, taps, bias):
    total = bias
    for tap in range(K):
        total = total + taps[tap : tap + 1] * ext[HALO - (K - 1) + tap : HALO - (K - 1) + tap + QB]
    return total


def split_maps(maps):
    return tuple(maps[:, N * index : N * (index + 1)] for index in range(4))


def scan_forward_kernel(
    place_ref, pre_ref, halo_ref, taps_ref, ssm_ref, skip_ref, spread_ref,
    conv_ref, mixed_ref, run_ref, delta_ref, ahead_ref, behind_ref, slope_ref,
    conv_all, behind_all, ahead_state, behind_state,
):
    blocks = pl.num_programs(0) // 2
    step = pl.program_id(0)

    @pl.when(step < blocks)
    def first_phase():
        block = blocks - 1 - step
        rows = pl.ds(pl.multiple_of(block * QB, QB), QB)
        kept = pl.ds(pl.multiple_of(block * 2 * N, 2 * N), 2 * N)

        @pl.when(step == 0)
        def start():
            behind_state[...] = jnp.zeros_like(behind_state)

        raw = pre_ref[:, CW:].astype(F32) + ssm_ref[0:1]
        delta = (jnp.maximum(raw, 0.0) + jnp.log1p(jnp.exp(-jnp.abs(raw)))) * keep_tile(place_ref[3], block)
        rates = -delta * ssm_ref[1:2]
        row = iota((QB, QB), 0)
        col = iota((QB, QB), 1)
        run = jnp.where(
            col < H,
            dot_exact((row >= col).astype(F32), rates),
            dot_exact((row <= col).astype(F32), rates),
        )
        run_ref[rows, :] = run
        delta_ref[rows, :] = delta
        edge = edge_row(run)
        scale = two_parts(delta * jnp.exp(edge - run))
        edge_exp = two_parts(jnp.broadcast_to(jnp.exp(edge), (8, QB)))

        def convolve(cols):
            halo = jnp.where(block > 0, halo_ref[:, cols].astype(F32), 0.0)
            ext = jnp.concatenate([halo, pre_ref[:, cols].astype(F32)], 0)
            total = conv_pieces(ext, taps_ref[:, cols], taps_ref[K : K + 1, cols])
            gate = sigmoid(total)
            value = (total * gate).astype(BF16)
            conv_ref[:, cols] = value
            conv_all[rows, cols] = value
            slope_ref[:, cols] = gate * (1.0 + total * (1.0 - gate))
            return value

        maps = convolve(slice(XW, CW))
        in_back = maps[:, 2 * N : 3 * N]
        in_back = jnp.concatenate([in_back, in_back], 0)
        for group in range(GROUPS):
            cols = lanes(group)
            wide_scale = dot(scale, spread_ref[:, back_lanes(group)])
            wide_edge = dot(edge_exp, spread_ref[:, back_lanes(group)])[0:1]
            state = behind_state[:, cols]
            low = jnp.concatenate(split(state), 0)
            behind_ref[:, cols] = low
            behind_all[kept, cols] = low
            pushed = jnp.concatenate(split(convolve(cols).astype(F32) * wide_scale), 0)
            behind_state[:, cols] = state * wide_edge + dot_tn(in_back, pushed)

    @pl.when(step >= blocks)
    def second_phase():
        block = step - blocks
        rows = pl.ds(pl.multiple_of(block * QB, QB), QB)
        kept = pl.ds(pl.multiple_of(block * 2 * N, 2 * N), 2 * N)

        @pl.when(step == blocks)
        def start():
            ahead_state[...] = jnp.zeros_like(ahead_state)

        in_fwd, out_fwd, in_back, out_back = split_maps(conv_all[rows, XW:])
        delta = delta_ref[rows, :]
        run = run_ref[rows, :]
        before = run + delta * ssm_ref[1:2]
        run_t = (run * LOG2_E).T
        before_two = before * LOG2_E
        delta_t = delta.T
        edge = edge_row(run)
        before_exp = two_parts(jnp.exp(before))
        scale = two_parts(delta * jnp.exp(edge - run))
        edge_exp = two_parts(jnp.broadcast_to(jnp.exp(edge), (8, QB)))
        lower, scores = block_scores(in_fwd, out_fwd, in_back, out_back)
        two_in = jnp.concatenate([in_fwd, in_fwd], 0)
        two_out_fwd = doubled(out_fwd)
        two_out_back = doubled(out_back)

        def products(group):
            cols = lanes(group)
            state = ahead_state[:, cols]
            low = jnp.concatenate(split(state), 0)
            ahead_ref[:, cols] = low
            return (
                state,
                dot(two_out_fwd, low),
                dot(two_out_back, behind_all[kept, cols]),
                dot(before_exp, spread_ref[:, cols]),
                dot(before_exp, spread_ref[:, back_lanes(group)]),
                dot(scale, spread_ref[:, cols]),
                dot(edge_exp, spread_ref[:, cols])[0:1],
            )

        ready = products(0)
        for group in range(GROUPS):
            state, carried_f, carried_b, wide_f, wide_b, wide_scale, wide_edge = ready
            if group + 1 < GROUPS:
                ready = products(group + 1)
            cols = lanes(group)
            values = conv_all[rows, cols]
            within = []
            for pair in range(2):
                weights = []
                for place in range(2):
                    head = group * GROUP_HEADS + 2 * pair + place
                    decay, size = decay_of(before_two, run_t, delta_t, lower, head)
                    weights.append(split(decay * scores * size))
                halved = halves(values[:, pair * QB : (pair + 1) * QB])
                weights = jnp.concatenate([weights[0][0], weights[1][0], weights[0][1], weights[1][1]], 1)
                within.append(dot(weights, jnp.concatenate([halved, halved], 0)))
            wide = values.astype(F32)
            mixed = jnp.concatenate(within, 1) + carried_f * wide_f + carried_b * wide_b
            mixed_ref[:, cols] = (mixed + wide * skip_ref[0:1, cols]).astype(BF16)
            pushed = jnp.concatenate(split(wide * wide_scale), 0)
            ahead_state[:, cols] = state * wide_edge + dot_tn(two_in, pushed)


def scan_backward_kernel(
    place_ref, grad_ref, conv_ref, pre_ref, slope_ref, run_ref, delta_ref, ahead_ref, behind_ref,
    taps_ref, ssm_ref, skip_ref, seg_ref, spread_ref,
    out_ref, other_ref, taps_grad_ref, ssm_grad_ref, skip_grad_ref,
    behind_grads, ahead_grad, behind_grad, col_rows, row_sums, next_rows,
):
    blocks = pl.num_programs(0) // 2
    step = pl.program_id(0)
    run = run_ref[...]
    delta = delta_ref[...]
    before = run + delta * ssm_ref[1:2]
    edge = edge_row(run)
    edge_exp = jnp.exp(edge)
    edge_parts = two_parts(jnp.broadcast_to(edge_exp, (8, QB)))
    before_exp = two_parts(jnp.exp(before))

    @pl.when(step < blocks)
    def first_phase():
        @pl.when(step == 0)
        def start():
            behind_grad[...] = jnp.zeros_like(behind_grad)

        kept = pl.ds(pl.multiple_of(step * 2 * N, 2 * N), 2 * N)
        out_back = conv_ref[:, XW + 3 * N : XW + 4 * N]
        for group in range(GROUPS):
            cols = lanes(group)
            state = behind_grad[:, cols]
            behind_grads[kept, cols] = jnp.concatenate(split(state), 0)
            wide = dot(before_exp, spread_ref[:, back_lanes(group)])
            wide_edge = dot(edge_parts, spread_ref[:, back_lanes(group)])[0:1]
            scaled = (grad_ref[:, cols].astype(F32) * wide).astype(BF16)
            behind_grad[:, cols] = state * wide_edge + dot_tn(out_back, scaled)

    @pl.when(step >= blocks)
    def second_phase():
        block = 2 * blocks - 1 - step
        kept = pl.ds(pl.multiple_of(block * 2 * N, 2 * N), 2 * N)

        @pl.when(step == blocks)
        def start():
            ahead_grad[...] = jnp.zeros_like(ahead_grad)
            taps_grad_ref[...] = jnp.zeros_like(taps_grad_ref)
            ssm_grad_ref[...] = jnp.zeros_like(ssm_grad_ref)
            skip_grad_ref[...] = jnp.zeros_like(skip_grad_ref)
            next_rows[...] = jnp.zeros_like(next_rows)
            col_rows[...] = jnp.zeros_like(col_rows)
            row_sums[...] = jnp.zeros_like(row_sums)

        lane = iota((QB, QB), 1)
        lane_row = iota((1, QB), 1)
        in_fwd, out_fwd, in_back, out_back = split_maps(conv_ref[:, XW:])
        run_t = (run * LOG2_E).T
        before_two = before * LOG2_E
        delta_t = delta.T
        to_edge = jnp.exp(edge - run)
        scale = delta * to_edge
        scale_parts = two_parts(scale)
        lower, scores = block_scores(in_fwd, out_fwd, in_back, out_back)
        two_out_fwd = doubled(out_fwd)
        two_out_back = doubled(out_back)
        two_in_fwd = doubled(in_fwd)
        two_in_back = doubled(in_back)

        def products(group):
            cols = lanes(group)
            state = ahead_grad[:, cols]
            ahead_low = jnp.concatenate(split(state), 0)
            behind_low = behind_grads[kept, cols]
            outer = [
                dot_nt(grad_ref[:, part], halves(conv_ref[:, part]))
                for part in (slice(base, base + QB) for base in range(cols.start, cols.stop, QB))
            ]
            return (
                outer,
                state,
                ahead_low[:N],
                behind_low[:N],
                dot(two_out_fwd, ahead_ref[:, cols]),
                dot(two_out_back, behind_ref[:, cols]),
                dot(two_in_fwd, ahead_low),
                dot(two_in_back, behind_low),
                dot(before_exp, spread_ref[:, cols]),
                dot(before_exp, spread_ref[:, back_lanes(group)]),
                dot(scale_parts, spread_ref[:, cols]),
                dot(scale_parts, spread_ref[:, back_lanes(group)]),
                dot(edge_parts, spread_ref[:, cols])[0:1],
            )

        def convolve(cols, value_grad):
            taps = taps_ref[:, cols]
            before_conv = pre_ref[:, cols].astype(F32)
            total_grad = value_grad.astype(F32) * slope_ref[:, cols]
            reach = jnp.concatenate([total_grad, next_rows[:, cols]], 0)
            taps_grad_ref[K : K + 1, cols] += jnp.sum(total_grad, 0, keepdims=True)
            result = jnp.zeros(before_conv.shape, F32)
            for tap in range(K):
                later = reach[K - 1 - tap : K - 1 - tap + QB]
                result = result + taps[tap : tap + 1] * later
                taps_grad_ref[tap : tap + 1, cols] += jnp.sum(before_conv * later, 0, keepdims=True)
            out_ref[:, cols] = result.astype(BF16)
            next_rows[:, cols] = total_grad[0:8]

        score_grad = jnp.zeros((QB, QB), F32)
        both_sums = jnp.zeros((2 * QB, QB), F32)
        out_fwd_grad = out_back_grad = in_fwd_grad = in_back_grad = jnp.zeros((QB, N), F32)
        held = jnp.zeros((1, QB), F32)
        ready = products(0)
        for group in range(GROUPS):
            (outer, state, ahead_low, behind_low, carried_f, carried_b, pulled_f, pulled_b,
             wide_f, wide_b, scale_f, scale_b, wide_edge) = ready
            if group + 1 < GROUPS:
                ready = products(group + 1)
            cols = lanes(group)
            values = conv_ref[:, cols]
            grads = grad_ref[:, cols]
            value_grad = []
            for pair in range(2):
                weights = []
                for place in range(2):
                    head = group * GROUP_HEADS + 2 * pair + place
                    decay, size = decay_of(before_two, run_t, delta_t, lower, head)
                    weights.append(split(decay * scores * size))
                    mixed = outer[pair][:, place * QB : (place + 1) * QB] * decay
                    score_grad = score_grad + mixed * size
                    direct = mixed * scores
                    direct_low = jnp.where(lower, direct, 0.0)
                    direct_sum = jnp.sum(direct, 0, keepdims=True)
                    direct_low_sum = jnp.sum(direct_low, 0, keepdims=True)
                    col_rows[head : head + 1, :] = direct_low_sum
                    col_rows[H + head : H + head + 1, :] = direct_sum - direct_low_sum
                    whole = direct * size
                    whole_sum = jnp.sum(whole, 1, keepdims=True)
                    whole_low_sum = jnp.sum(jnp.where(lower, whole, 0.0), 1, keepdims=True)
                    row_sums[:, head : head + 1] = whole_low_sum
                    row_sums[:, H + head : H + head + 1] = whole_sum - whole_low_sum
                halved = halves(grads[:, pair * QB : (pair + 1) * QB])
                weights = jnp.concatenate([weights[0][0], weights[1][0], weights[0][1], weights[1][1]], 0)
                value_grad.append(dot_tn(weights, jnp.concatenate([halved, halved], 0)))
            wide = values.astype(F32)
            wide_grad = grads.astype(F32)
            scaled_f = wide_grad * wide_f
            scaled_b = wide_grad * wide_b
            sums_f = jnp.concatenate([scaled_f * carried_f, wide * pulled_f], 0).astype(BF16)
            sums_b = jnp.concatenate([scaled_b * carried_b, wide * pulled_b], 0).astype(BF16)
            both_sums = both_sums + dot(sums_f, seg_ref[cols, :]) + dot(sums_b, seg_ref[back_lanes(group), :])
            scaled_f = scaled_f.astype(BF16)
            scaled_b = scaled_b.astype(BF16)
            ahead_in = ahead_ref[:N, cols]
            behind_in = behind_ref[:N, cols]
            out_fwd_grad = out_fwd_grad + dot_nt(scaled_f, ahead_in)
            out_back_grad = out_back_grad + dot_nt(scaled_b, behind_in)
            in_fwd_grad = in_fwd_grad + dot_nt((wide * scale_f).astype(BF16), ahead_low)
            in_back_grad = in_back_grad + dot_nt((wide * scale_b).astype(BF16), behind_low)
            result = jnp.concatenate(value_grad, 1) + scale_f * pulled_f + scale_b * pulled_b
            result = result + wide_grad * skip_ref[0:1, cols]
            ahead_grad[:, cols] = state * wide_edge + dot_tn(out_fwd, scaled_f)
            skip_grad_ref[0:1, cols] += jnp.sum(wide * wide_grad, 0, keepdims=True)
            for low, kept_state, shift in ((ahead_low, ahead_in, 0), (behind_low, behind_in, H)):
                product = jnp.sum(low.astype(F32) * kept_state.astype(F32), 0, keepdims=True)
                for pair in range(2):
                    part = product[:, pair * QB : (pair + 1) * QB]
                    for place in range(2):
                        inside = (lane_row < P_SIZE) if place == 0 else (lane_row >= P_SIZE)
                        total = jnp.sum(jnp.where(inside, part, 0.0), 1, keepdims=True)
                        held = jnp.where(lane_row == shift + group * GROUP_HEADS + 2 * pair + place, total, held)
            convolve(cols, result.astype(BF16))
        for part in split(jnp.where(iota((QB, QB), 0) > lane, score_grad, 0.0)):
            out_fwd_grad = out_fwd_grad + dot(part, in_fwd)
            in_fwd_grad = in_fwd_grad + dot_tn(part, out_fwd)
        for part in split(jnp.where(iota((QB, QB), 0) < lane, score_grad, 0.0)):
            out_back_grad = out_back_grad + dot(part, in_back)
            in_back_grad = in_back_grad + dot_tn(part, out_back)
        map_grads = jnp.concatenate([in_fwd_grad, out_fwd_grad, in_back_grad, out_back_grad], 1)
        convolve(slice(XW, CW), map_grads.astype(BF16))

        direct = col_rows[...].T
        column = delta * direct
        reached = both_sums[QB:]
        weighted = row_sums[...] + both_sums[:QB] - column
        entered = scale * reached
        first = jnp.where(lane < H, weighted, entered)
        second = jnp.where(lane < H, entered, weighted)
        row = iota((QB, QB), 0)
        rate_grad = dot_exact((row < lane).astype(F32), first) + dot_exact((row > lane).astype(F32), second)
        rate_grad = rate_grad - column + held * edge_exp
        delta_grad = direct + to_edge * reached - rate_grad * ssm_ref[1:2]
        raw = pre_ref[:, CW:].astype(F32) + ssm_ref[0:1]
        raw_grad = delta_grad * keep_tile(place_ref[3], block) * sigmoid(raw)
        ssm_grad_ref[0:1, :] += jnp.sum(raw_grad, 0, keepdims=True)
        ssm_grad_ref[1:2, :] += jnp.sum(rate_grad * (delta * -ssm_ref[1:2]), 0, keepdims=True)
        out_ref[:, CW:] = raw_grad.astype(BF16)
        for chip in range(2):
            col = pl.multiple_of((2 * chip + 1 - place_ref[2]) * TILE, QB)
            other_ref[:, chip * TILE : (chip + 1) * TILE] = out_ref[:, pl.ds(col, TILE)]
        other_ref[:, 2 * TILE :] = out_ref[:, XW:]

        @pl.when(block == 0)
        def finish():
            skip_heads = jnp.zeros((8, QB), F32)
            for part in split(jnp.broadcast_to(skip_grad_ref[0:1, :], (8, XW))):
                skip_heads = skip_heads + dot(part, seg_ref[:XW, :])
            ssm_grad_ref[2:3, :] = (
                ssm_grad_ref[0:1, :]
                + pltpu.roll(ssm_grad_ref[1:2, :], 2 * H, 1)
                + pltpu.roll(skip_heads[0:1], 4 * H, 1)
            )


def whole_spec(shape):
    return pl.BlockSpec(shape, lambda step: (0,) * len(shape))


def scan_forward(place, pre, taps, ssm, skip):
    total = pre.shape[0]
    blocks = total // QB

    def first(step):
        return jnp.maximum(blocks - 1 - step, 0)

    def second(step):
        return jnp.maximum(step - blocks, 0)

    per = QB // HALO
    return pl.pallas_call(
        scan_forward_kernel,
        grid=(2 * blocks,),
        in_specs=[
            pl.BlockSpec(memory_space=pltpu.SMEM),
            pl.BlockSpec((QB, PW), lambda step: (first(step), 0)),
            pl.BlockSpec((HALO, PW), lambda step: (jnp.maximum(first(step) * per - 1, 0), 0)),
            whole_spec((8, CW)),
            whole_spec((8, QB)),
            whole_spec((8, XW)),
            whole_spec((2 * QB, 2 * XW)),
        ],
        out_specs=[
            pl.BlockSpec((QB, CW), lambda step: (first(step), 0)),
            pl.BlockSpec((QB, XW), lambda step: (second(step), 0)),
            whole_spec((total, QB)),
            whole_spec((total, QB)),
            pl.BlockSpec((2 * N, XW), lambda step: (second(step), 0)),
            pl.BlockSpec((2 * N, XW), lambda step: (first(step), 0)),
            pl.BlockSpec((QB, CW), lambda step: (first(step), 0)),
        ],
        out_shape=[
            jax.ShapeDtypeStruct((total, CW), BF16),
            jax.ShapeDtypeStruct((total, XW), BF16),
            jax.ShapeDtypeStruct((total, QB), F32),
            jax.ShapeDtypeStruct((total, QB), F32),
            jax.ShapeDtypeStruct((2 * blocks * N, XW), BF16),
            jax.ShapeDtypeStruct((2 * blocks * N, XW), BF16),
            jax.ShapeDtypeStruct((total, CW), F32),
        ],
        scratch_shapes=[
            pltpu.VMEM((total, CW), BF16),
            pltpu.VMEM((2 * blocks * N, XW), BF16),
            pltpu.VMEM((N, XW), F32),
            pltpu.VMEM((N, XW), F32),
        ],
        compiler_params=pltpu.CompilerParams(vmem_limit_bytes=VMEM_BYTES),
        cost_estimate=pl.CostEstimate(flops=26000 * total * XW, bytes_accessed=1, transcendentals=0),
        name="scan_forward",
    )(place, pre, pre, taps, ssm, skip, spread_matrix())


def scan_backward(device, grads, conv_low, pre, slope, run, delta, ahead, behind, taps, ssm, skip):
    total = pre.shape[0]
    blocks = total // QB

    def place(step):
        return jnp.where(step < blocks, step, 2 * blocks - 1 - step)

    def late(step):
        return jnp.minimum(2 * blocks - 1 - step, blocks - 1)

    places = np.arange(2 * XW)[:, None]
    segment = np.arange(QB)[None] == H * (places // XW) + places % XW // P_SIZE
    segment = jnp.asarray(segment, BF16)
    row_block = lambda width, where: pl.BlockSpec((QB, width), lambda step: (where(step), 0))
    return pl.pallas_call(
        scan_backward_kernel,
        grid=(2 * blocks,),
        in_specs=[
            pl.BlockSpec(memory_space=pltpu.SMEM),
            row_block(XW, place),
            row_block(CW, place),
            row_block(PW, late),
            row_block(CW, late),
            row_block(QB, place),
            row_block(QB, place),
            pl.BlockSpec((2 * N, XW), lambda step: (late(step), 0)),
            pl.BlockSpec((2 * N, XW), lambda step: (late(step), 0)),
            whole_spec((8, CW)),
            whole_spec((8, QB)),
            whole_spec((8, XW)),
            whole_spec((2 * XW, QB)),
            whole_spec((2 * QB, 2 * XW)),
        ],
        out_specs=[
            row_block(PW, late),
            row_block(3 * TILE, late),
            whole_spec((8, CW)),
            whole_spec((8, QB)),
            whole_spec((8, XW)),
        ],
        out_shape=[
            jax.ShapeDtypeStruct((total, PW), BF16),
            jax.ShapeDtypeStruct((total, 3 * TILE), BF16),
            jax.ShapeDtypeStruct((8, CW), F32),
            jax.ShapeDtypeStruct((8, QB), F32),
            jax.ShapeDtypeStruct((8, XW), F32),
        ],
        scratch_shapes=[
            pltpu.VMEM((2 * blocks * N, XW), BF16),
            pltpu.VMEM((N, XW), F32),
            pltpu.VMEM((N, XW), F32),
            pltpu.VMEM((QB, QB), F32),
            pltpu.VMEM((QB, QB), F32),
            pltpu.VMEM((8, CW), F32),
        ],
        compiler_params=pltpu.CompilerParams(vmem_limit_bytes=VMEM_BYTES),
        cost_estimate=pl.CostEstimate(flops=48000 * total * XW, bytes_accessed=1, transcendentals=0),
        name="scan_backward",
    )(device, grads, conv_low, pre, slope, run, delta, ahead, behind, taps, ssm, skip, segment, spread_matrix())


TILE = 384
SEQS, CHIPS = 4, 4
ROWS_ZX, ROWS_OUT, ROWS_BC = D // SEQS, D // 8, 48
PIECE = 2 * ROWS_ZX + CHIPS // 2 * ROWS_BC
REST = 2 * ROWS_ZX + CHIPS * ROWS_OUT
BC_COLS = MW + 2 * H
BC_EACH = BC_COLS // 8
BC_LANES = 256
SMALL_EDGES = (0, K * CW, K * CW + D, K * CW + D + E, K * CW + D + E + CW, K * CW + D + E + CW + 5 * H)
SMALL_ROWS = 96
CONV_ROWS = K * CW // QB
CHUNK_ROW = 40
BLOCK = 256


def small_maps():
    inner = np.arange(8 * ROWS_BC)[None]
    std = np.arange(TILE)[:, None]
    row_map = (inner % ROWS_BC < BC_EACH) & (std == inner // ROWS_BC * BC_EACH + inner % ROWS_BC)
    inner = np.arange(SEQS * BC_LANES)[:, None]
    std = np.arange(D)[None]
    col_map = (inner % BC_LANES < ROWS_ZX) & (std == inner // BC_LANES * ROWS_ZX + inner % BC_LANES)
    return jnp.asarray(row_map, BF16), jnp.asarray(col_map, BF16)


def whole(shape):
    return pl.BlockSpec(shape, lambda *index: (0,) * len(shape))


def scalar_call(kernel, scalars, grid, inputs, in_specs, outs, out_specs, scratch=(), name=None, flops=1):
    spec = pltpu.PrefetchScalarGridSpec(
        num_scalar_prefetch=1, grid=grid, in_specs=in_specs, out_specs=out_specs, scratch_shapes=scratch
    )
    return pl.pallas_call(
        kernel,
        grid_spec=spec,
        out_shape=outs,
        compiler_params=pltpu.CompilerParams(vmem_limit_bytes=VMEM_BYTES),
        cost_estimate=pl.CostEstimate(flops=flops, bytes_accessed=1, transcendentals=0),
        name=name,
    )(scalars, *inputs)


def small_rows(chip):
    start = 2 * ROWS_ZX + chip // 2 * ROWS_BC
    return slice(start, start + ROWS_BC)


def half_row(value, chip):
    return pltpu.roll(value, ROWS_ZX, 1) if chip % 2 else value


def seq_rows(place, index, rows):
    return pl.ds(pl.multiple_of((place[0] ^ index) * rows, rows), rows)


def join_columns(place, refs, out_ref):
    for core in range(2):
        for index in range(SEQS):
            for chip in range(2):
                tile = 2 * ((place[1] & 1) ^ chip) + (place[2] ^ core)
                cols = pl.ds(pl.multiple_of(tile * TILE, QB), TILE)
                piece = refs[SEQS * core + index][chip * ROWS_ZX : (chip + 1) * ROWS_ZX, :]
                out_ref[seq_rows(place, index, ROWS_ZX), cols] = piece


def join_out(place, refs, out_ref):
    for index in range(SEQS):
        cols = pl.ds(pl.multiple_of((place[0] ^ index) * TILE, QB), TILE)
        for core in range(2):
            for chip in range(CHIPS):
                tok = 2 * (chip ^ place[1]) + (core ^ place[2])
                rows = pl.ds(pl.multiple_of(tok * ROWS_OUT, ROWS_OUT), ROWS_OUT)
                row = 2 * ROWS_ZX + chip * ROWS_OUT
                out_ref[rows, cols] = refs[SEQS * core + index][row : row + ROWS_OUT, :]


def join_weights(scalars, pieces):
    row_map, col_map = small_maps()

    def kernel(place, row_ref, col_ref, *refs):
        refs, (wide_ref, small_ref, small_pieces) = refs[: 2 * SEQS], refs[2 * SEQS :]
        join_columns(place, refs, wide_ref)
        for core in range(2):
            for index in range(SEQS):
                cols = pl.ds(pl.multiple_of((place[0] ^ index) * BC_LANES, BC_LANES), BC_LANES)
                for chip in range(CHIPS):
                    tok = 2 * (chip ^ place[1]) + (core ^ place[2])
                    rows = pl.ds(pl.multiple_of(tok * ROWS_BC, ROWS_BC), ROWS_BC)
                    piece = refs[SEQS * core + index][small_rows(chip), :].astype(F32)
                    small_pieces[rows, cols] = half_row(piece, chip)[:, :BC_LANES].astype(BF16)
        rows = dot(row_ref[...], small_pieces[...]).astype(BF16)
        small_ref[...] = dot(rows, col_ref[...]).astype(BF16)

    return scalar_call(
        kernel, scalars, (1,), (row_map, col_map, *pieces),
        [whole(row_map.shape), whole(col_map.shape)] + [whole((PIECE, TILE))] * (2 * SEQS),
        [jax.ShapeDtypeStruct((D, XW), BF16), jax.ShapeDtypeStruct((TILE, D), BF16)],
        [whole((D, XW)), whole((TILE, D))],
        scratch=[pltpu.VMEM((8 * ROWS_BC, SEQS * BC_LANES), BF16)],
        name="join_weights",
    )


def project(hidden, gain_in, inner_weights, small_weights):
    total = hidden.shape[0]

    def kernel(hidden_ref, gain_ref, wide_ref, small_ref, normed_ref, normed_t_ref, pre_ref):
        value = hidden_ref[...].astype(F32)
        scale = lax.rsqrt(jnp.mean(value * value, -1, keepdims=True) + NORM_EPS)
        normed = (value * scale * gain_ref[0:1]).astype(BF16)
        normed_ref[...] = normed
        normed_t_ref[...] = normed.T
        pre_ref[:, :XW] = dot(normed, wide_ref[...]).astype(BF16)
        pre_ref[:, XW:] = dot_nt(normed, small_ref[...]).astype(BF16)

    def rows(width):
        return pl.BlockSpec((BLOCK, width), lambda step: (step, 0))

    return pl.pallas_call(
        kernel,
        grid=(total // BLOCK,),
        in_specs=[rows(D), whole((8, D)), whole((D, XW)), whole((TILE, D))],
        out_specs=[rows(D), pl.BlockSpec((D, BLOCK), lambda step: (0, step)), rows(PW)],
        out_shape=[
            jax.ShapeDtypeStruct((total, D), BF16),
            jax.ShapeDtypeStruct((D, total), BF16),
            jax.ShapeDtypeStruct((total, PW), BF16),
        ],
        compiler_params=pltpu.CompilerParams(vmem_limit_bytes=VMEM_BYTES),
        cost_estimate=pl.CostEstimate(flops=8 * total * D * PW, bytes_accessed=1, transcendentals=0),
        name="project",
    )(hidden, gain_in, inner_weights, small_weights)


def gated_norm(scalars, normed, mixed, hidden, upstream, gain_out, pieces):
    total = hidden.shape[0]

    def kernel(place, normed_ref, mixed_ref, hidden_ref, upstream_ref, gain_ref, *refs):
        pieces, refs = refs[: 2 * SEQS], refs[2 * SEQS :]
        (hidden_out_ref, gated_ref, mixed_grad_ref, gate_grad_ref, branch_t_ref, gain_grad_ref, gate_w, out_w) = refs
        step = pl.program_id(0)

        @pl.when(step == 0)
        def start():
            gain_grad_ref[...] = jnp.zeros_like(gain_grad_ref)
            join_columns(place, pieces, gate_w)
            join_out(place, pieces, out_w)

        keep = jnp.where(step * BLOCK + iota((BLOCK, 1), 0) < place[3], 1.0, 0.0).astype(F32)
        gain = gain_ref[0:1]
        branch_grad = (upstream_ref[...].astype(F32) * keep).astype(BF16)
        branch_t_ref[...] = branch_grad.T
        gated_grad = dot(branch_grad, out_w[...])
        gate_in = dot(normed_ref[...], gate_w[...])
        sig = sigmoid(gate_in)
        gate = gate_in * sig
        mixed = mixed_ref[...].astype(F32)
        gated = mixed * gate
        scale = lax.rsqrt(jnp.mean(gated * gated, -1, keepdims=True) + NORM_EPS)
        unit = gated * scale
        gated_low = (unit * gain).astype(BF16)
        gated_ref[...] = gated_low
        branch = dot_nt(gated_low, out_w[...])
        hidden_out_ref[...] = (hidden_ref[...].astype(F32) + keep * branch).astype(BF16)
        gain_grad_ref[0:1] += jnp.sum(gated_grad * unit, 0, keepdims=True)
        pulled = gated_grad * gain
        inner = scale * (pulled - unit * jnp.mean(pulled * unit, -1, keepdims=True))
        mixed_grad_ref[...] = (inner * gate).astype(BF16)
        gate_grad_ref[...] = (inner * mixed * (sig * (1.0 + gate_in * (1.0 - sig)))).astype(BF16)

    def rows(width):
        return pl.BlockSpec((BLOCK, width), lambda step, place: (step, 0))

    return scalar_call(
        kernel, scalars, (total // BLOCK,),
        (normed, mixed, hidden, upstream, gain_out, *pieces),
        [rows(D), rows(E), rows(D), rows(D), whole((8, E))]
        + [whole((REST, TILE))] * (2 * SEQS),
        [
            jax.ShapeDtypeStruct((total, D), BF16),
            jax.ShapeDtypeStruct((total, E), BF16),
            jax.ShapeDtypeStruct((total, E), BF16),
            jax.ShapeDtypeStruct((total, E), BF16),
            jax.ShapeDtypeStruct((D, total), BF16),
            jax.ShapeDtypeStruct((8, E), F32),
            jax.ShapeDtypeStruct((D, E), BF16),
        ],
        [rows(D), rows(E), rows(E), rows(E), pl.BlockSpec((D, BLOCK), lambda step, place: (0, step)), whole((8, E)),
         whole((D, E))],
        scratch=[pltpu.VMEM((D, E), BF16)],
        name="gated_norm",
        flops=19 * total * D * E,
    )


def input_grad(gate_grad, pre_grad, hidden, upstream, gain_in, inner_weights, small_weights, gate_weights, early):
    total = hidden.shape[0]
    count = len(early)

    def kernel(gate_ref, pre_ref, hidden_ref, upstream_ref, gain_ref, inner_w, small_w, gate_w, *refs):
        early_refs, (out_ref, gain_grad_ref, *sums) = refs[:count], refs[count:]

        @pl.when(pl.program_id(0) == 0)
        def start():
            gain_grad_ref[...] = jnp.zeros_like(gain_grad_ref)

        for core, ref in enumerate(sums):
            ref[...] = sum(early_ref[core].astype(F32) for early_ref in early_refs)
        grad = dot(pre_ref[:, XW:], small_w[...])
        grad = grad + dot_nt(pre_ref[:, :XW], inner_w[...])
        grad = grad + dot_nt(gate_ref[...], gate_w[...])
        value = hidden_ref[...].astype(F32)
        scale = lax.rsqrt(jnp.mean(value * value, -1, keepdims=True) + NORM_EPS)
        unit = value * scale
        gain_grad_ref[0:1] += jnp.sum(grad * unit, 0, keepdims=True)
        pulled = grad * gain_ref[0:1]
        inner = scale * (pulled - unit * jnp.mean(pulled * unit, -1, keepdims=True))
        out_ref[...] = (upstream_ref[...].astype(F32) + inner).astype(BF16)

    steps = total // BLOCK

    def rows(width):
        return pl.BlockSpec((BLOCK, width), lambda step: (step, 0))

    outs = [jax.ShapeDtypeStruct((total, D), BF16), jax.ShapeDtypeStruct((8, D), F32)]
    out_specs = [rows(D), whole((8, D))]
    if early:
        outs += [jax.ShapeDtypeStruct((REST, TILE), F32)] * 2
        out_specs += [pl.BlockSpec((REST // steps, TILE), lambda step: (step, 0))] * 2
    return pl.pallas_call(
        kernel,
        grid=(steps,),
        in_specs=[rows(E), rows(PW), rows(D), rows(D), whole((8, D)), whole((D, XW)), whole((TILE, D)), whole((D, E))]
        + [pl.BlockSpec((2, REST // steps, TILE), lambda step: (0, step, 0))] * count,
        out_specs=out_specs,
        out_shape=outs,
        compiler_params=pltpu.CompilerParams(vmem_limit_bytes=VMEM_BYTES),
        cost_estimate=pl.CostEstimate(flops=1, bytes_accessed=1, transcendentals=0),
        name="input_grad",
    )(gate_grad, pre_grad, hidden, upstream, gain_in, inner_weights, small_weights, gate_weights, *early)


def early_grads(scalars, normed_t, gate_grad, branch_t, gated_low):
    total = normed_t.shape[1]

    def kernel(place, normed_ref, gate_ref, branch_ref, gated_ref, *refs):
        outs, value_ref = refs[:SEQS], refs[SEQS]
        step = pl.program_id(0)

        @pl.when(step < 2)
        def gates():
            value_ref[...] = dot(normed_ref[...], gate_ref[...]).astype(BF16)
            rows = pl.ds(pl.multiple_of((step ^ (place[1] & 1)) * ROWS_ZX, ROWS_ZX), ROWS_ZX)
            for index in range(SEQS):
                source = seq_rows(place, index, ROWS_ZX)
                for core in range(2):
                    outs[index][core ^ place[2], rows, :] = value_ref[source, core * TILE : (core + 1) * TILE]

        @pl.when(step >= 2)
        def weights():
            value_ref[...] = dot(branch_ref[...], gated_ref[...]).astype(BF16)
            for index in range(SEQS):
                seq = place[0] ^ index

                @pl.when(seq // 2 == step - 2)
                def store():
                    cols = pl.ds(pl.multiple_of((seq % 2) * TILE, QB), TILE)
                    for tok in range(8):
                        row = 2 * ROWS_ZX + ((tok >> 1) ^ place[1]) * ROWS_OUT
                        rows = pl.ds(pl.multiple_of(row, ROWS_OUT), ROWS_OUT)
                        outs[index][(tok & 1) ^ place[2], rows, :] = value_ref[
                            tok * ROWS_OUT : (tok + 1) * ROWS_OUT, cols
                        ]

    shape = (2, 2 * ROWS_ZX + CHIPS * ROWS_OUT, TILE)
    return scalar_call(
        kernel, scalars, (4,), (normed_t, gate_grad, branch_t, gated_low),
        [
            whole((D, total)),
            pl.BlockSpec((total, 2 * TILE), lambda step, place: (0, jnp.minimum(step, 1))),
            whole((D, total)),
            pl.BlockSpec((total, 2 * TILE), lambda step, place: (0, jnp.maximum(step - 2, 0))),
        ],
        [jax.ShapeDtypeStruct(shape, BF16)] * SEQS,
        [whole(shape)] * SEQS,
        scratch=[pltpu.VMEM((D, 2 * TILE), BF16)],
        name="early_grads",
    )


def small_gradients(taps_ref, gain_in_ref, gain_out_ref, ssm_ref, out_ref):
    out_ref[...] = jnp.zeros_like(out_ref)
    line = 0
    for ref, source in [(taps_ref, tap) for tap in range(K)] + [
        (gain_in_ref, 0), (gain_out_ref, 0), (taps_ref, K), (ssm_ref, 2),
    ]:
        for base in range(0, ref.shape[1], QB):
            row, col = line // 3, line % 3 * QB
            out_ref[row : row + 1, col : col + QB] = ref[source : source + 1, base : base + QB]
            line += 1


def late_grads(scalars, normed_t, pre_grad, sibling_t, sibling_grad, smalls):
    total = normed_t.shape[1]
    steps = total // BLOCK
    row_map, col_map = small_maps()

    def kernel(
        place, own_t_ref, other_t_ref, grad_ref, other_ref, row_ref, col_ref, taps_ref, gain_in_ref, gain_out_ref, ssm_ref,
        *refs,
    ):
        outs, (vector_ref, wide_sum, small_sum, small_value) = refs[:SEQS], refs[SEQS:]
        step = pl.program_id(0)

        @pl.when(step == 0)
        def start():
            wide_sum[...] = jnp.zeros_like(wide_sum)
            small_sum[...] = jnp.zeros_like(small_sum)

        both_t = jnp.concatenate([own_t_ref[...], other_t_ref[...]], 1)
        tiles = []
        for chip in range(2):
            col = pl.multiple_of((2 * chip + place[2]) * TILE, QB)
            tile = [grad_ref[:, pl.ds(col, TILE)], other_ref[:, chip * TILE : (chip + 1) * TILE]]
            tiles.append(jnp.concatenate(tile, 0))
        wide_sum[...] += dot(both_t, jnp.concatenate(tiles, 1))
        small = jnp.concatenate([grad_ref[:, XW:], other_ref[:, 2 * TILE :]], 0)
        small_sum[...] += dot_nt(small.T, both_t)

        @pl.when(step == steps - 1)
        def finish():
            small_gradients(taps_ref, gain_in_ref, gain_out_ref, ssm_ref, vector_ref)
            result = jnp.zeros((8 * ROWS_BC, SEQS * BC_LANES), F32)
            for part in split(small_sum[...]):
                result = result + dot_nt(dot_tn(row_ref[...], part).astype(BF16), col_ref[...])
            small_value[...] = result
            line = iota((ROWS_BC, TILE), 0)
            rest = jnp.zeros((ROWS_BC, TILE - BC_LANES), F32)
            for index in range(SEQS):
                source = seq_rows(place, index, ROWS_ZX)
                for chip in range(2):
                    cols = pl.ds(pl.multiple_of((chip ^ (place[1] & 1)) * TILE, QB), TILE)
                    outs[index][chip * ROWS_ZX : (chip + 1) * ROWS_ZX, :] = wide_sum[source, cols].astype(BF16)
                cols = pl.ds(pl.multiple_of((place[0] ^ index) * BC_LANES, BC_LANES), BC_LANES)
                for pair in range(CHIPS // 2):
                    value = jnp.zeros((ROWS_BC, TILE), F32)
                    chunks = []
                    for chip in (2 * pair, 2 * pair + 1):
                        tok = 2 * (chip ^ place[1]) + place[2]
                        rows = pl.ds(pl.multiple_of(tok * ROWS_BC, ROWS_BC), ROWS_BC)
                        value = value + half_row(jnp.concatenate([small_value[rows, cols], rest], 1), chip)
                        for core in range(2):
                            device = (place[0] ^ index) * 8 + (tok ^ core)
                            chunks.extend(split(vector_ref[pl.ds(device, 1), :]))
                    for number, chunk in enumerate(chunks):
                        value = jnp.where(line == CHUNK_ROW + number, chunk.astype(F32), value)
                    outs[index][small_rows(2 * pair), :] = value.astype(BF16)

    piece = jax.ShapeDtypeStruct((PIECE, TILE), BF16)
    columns = pl.BlockSpec((D, BLOCK), lambda step, place: (0, step))

    def rows(width):
        return pl.BlockSpec((BLOCK, width), lambda step, place: (step, 0))

    return scalar_call(
        kernel, scalars, (steps,), (normed_t, sibling_t, pre_grad, sibling_grad, row_map, col_map, *smalls),
        [columns, columns, rows(PW), rows(3 * TILE), whole(row_map.shape), whole(col_map.shape)]
        + [whole(value.shape) for value in smalls],
        [piece] * SEQS,
        [whole(piece.shape)] * SEQS,
        scratch=[
            pltpu.VMEM((8 * SEQS, TILE), F32),
            pltpu.VMEM((D, 2 * TILE), F32),
            pltpu.VMEM((TILE, D), F32),
            pltpu.VMEM((8 * ROWS_BC, SEQS * BC_LANES), F32),
        ],
        name="late_grads",
    )


def whole_call(kernel, inputs, outs, name):
    return pl.pallas_call(
        kernel,
        grid=(1,),
        in_specs=[whole(value.shape) for value in inputs],
        out_specs=[whole(out.shape) for out in outs],
        out_shape=outs,
        compiler_params=pltpu.CompilerParams(vmem_limit_bytes=VMEM_BYTES),
        name=name,
    )(*inputs)


def matrices_step(parts, starts, zx, bc, out, devices):
    (rows_bc_t, cols_bc_t), (rows_out_t, cols_out_t) = bc[0].shape, out[0].shape
    count = len(parts)

    def kernel(*refs):
        part_refs, states, outs = refs[:count], refs[count : count + 9], refs[count + 9 :]

        def total(start, rows):
            return sum(ref[start : start + rows, :].astype(F32) for ref in part_refs)

        small = total(starts[1], starts[2] - starts[1])
        grads = (
            total(0, zx[0].shape[0]),
            small[:rows_bc_t, :cols_bc_t],
            total(starts[2], rows_out_t)[:, :cols_out_t],
        )
        lane = iota((1, QB), 1)
        row = jnp.zeros((1, QB), F32)
        for index, grad in enumerate(grads):
            param, first, second = (ref[...] for ref in states[3 * index : 3 * index + 3])
            first_new, second_new, direction = adam_step(param, grad, first, second)
            outs[3 * index][...] = first_new
            outs[3 * index + 1][...] = second_new
            outs[3 * index + 2][...] = direction
            for slot, value in ((index, param), (3 + index, direction)):
                square = jnp.sum(jnp.sum(value * value, 1, keepdims=True), 0, keepdims=True)
                row = jnp.where(lane == slot, square, row)
        chunks = [jnp.zeros((1, TILE), F32)] * 2
        if small.shape[0] > CHUNK_ROW:
            chunks = [small[first : first + 1] + small[first + 1 : first + 2] for first in (CHUNK_ROW, CHUNK_ROW + 2)]
        outs[9][...] = jnp.broadcast_to(jnp.concatenate([row, *chunks], 1)[None], (devices, 1, QB + 2 * TILE))

    arrays = [*zx, *bc, *out]
    outs = [jax.ShapeDtypeStruct(value.shape, F32) for value in arrays]
    outs.append(jax.ShapeDtypeStruct((devices, 1, QB + 2 * TILE), F32))
    return whole_call(kernel, [*parts, *arrays], outs, "matrices_step")


def pack_rows(parts):
    rows = [0]
    for part in parts:
        rows.append(rows[-1] + part.shape[0])

    def kernel(*refs):
        for index, ref in enumerate(refs[:-1]):
            refs[-1][rows[index] : rows[index + 1], :] = ref[...]

    return whole_call(kernel, parts, [jax.ShapeDtypeStruct((rows[-1], TILE), BF16)], "pack_rows")[0]


def chip_pieces(scalars, late, rest, rest_arrived):
    def kernel(place, *refs):
        late_refs, (own_ref, other_ref), outs = refs[:SEQS], refs[SEQS : SEQS + 2], refs[SEQS + 2 :]
        low = place[1] < 2
        line = iota((ROWS_BC, TILE), 0)
        for index in range(CHIPS):
            rows = slice(index % 2 * ROWS_ZX, (index % 2 + 1) * ROWS_ZX)
            inner = sum(ref[rows, :].astype(F32) for ref in late_refs)
            gates = own_ref[rows, :] + other_ref[rows, :]
            inner, gates = (inner, gates) if index >= 2 else (gates, inner)
            outs[index][:ROWS_ZX, :] = jnp.where(low, inner, gates).astype(BF16)
            both = sum(ref[small_rows(index), :].astype(F32) for ref in late_refs)
            small = half_row(both, index)
            for core in range(2):
                source, first = CHUNK_ROW + 4 * (index % 2) + 2 * core, CHUNK_ROW + 2 * core
                chunk = both[source : source + 1] + both[source + 1 : source + 2]
                rest = chunk - chunk.astype(BF16).astype(F32)
                small = jnp.where(line == first, chunk, jnp.where(line == first + 1, rest, small))
            outs[index][ROWS_ZX : ROWS_ZX + ROWS_BC, :] = small.astype(BF16)
            rows = slice(2 * ROWS_ZX + index * ROWS_OUT, 2 * ROWS_ZX + (index + 1) * ROWS_OUT)
            outs[index][ROWS_ZX + ROWS_BC :, :] = (own_ref[rows, :] + other_ref[rows, :]).astype(BF16)

    shape = (ROWS_ZX + ROWS_BC + ROWS_OUT, TILE)
    return scalar_call(
        kernel, scalars, (1,), (*late, rest, rest_arrived),
        [whole(value.shape) for value in (*late, rest, rest_arrived)],
        [jax.ShapeDtypeStruct(shape, BF16)] * CHIPS,
        [whole(shape)] * CHIPS,
        name="chip_pieces",
    )


def settle(value, name):
    rows = value.shape[1]

    def kernel(value_ref, out_ref):
        out_ref[...] = value_ref[...]

    return pl.pallas_call(
        kernel,
        grid=(value.shape[0] // 2,),
        in_specs=[pl.BlockSpec((2, rows, D), lambda step: (step, 0, 0))],
        out_specs=pl.BlockSpec((2, rows, D), lambda step: (step, 0, 0)),
        out_shape=jax.ShapeDtypeStruct(value.shape, value.dtype),
        name=name,
    )(value)


def last_step(squares, gathered, params, directions, conv, vec):
    def kernel(squares_ref, gathered_ref, *refs):
        conv_refs, vec_refs, refs = refs[6:9], refs[9:12], refs[:6] + refs[12:]
        outs = refs[9:]
        total = jnp.sum(squares_ref[:, :, :QB], 0)
        for index in range(3):
            ratio = jnp.sqrt(total[:, index : index + 1]) / jnp.sqrt(total[:, 3 + index : 4 + index] + UPDATE_EPS)
            refs[6 + index][...] = refs[index][...] - LEARN_RATE * ratio * refs[3 + index][...]
        lines = []
        for line in range(SMALL_ROWS):
            device, base = line // 3, (line % 3 + 1) * QB
            own = gathered_ref[device, :, base : base + QB]
            lines.append(own + gathered_ref[device ^ 1, :, TILE + base : TILE + base + QB])
        grad = jnp.concatenate(lines, 0)

        def rows_of(conv_ref, vec_ref):
            lines = [conv_ref[tap : tap + 1, base : base + QB] for tap in range(K) for base in range(0, CW, QB)]
            return jnp.concatenate([*lines, vec_ref[...]], 0)

        value, first, second = (rows_of(conv_refs[index], vec_refs[index]) for index in range(3))
        first_new, second_new, direction = adam_step(value, grad, first, second)
        where = iota(value.shape, 0) * QB + iota(value.shape, 1)
        lane = iota((1, 8), 1)
        rows = [jnp.concatenate([total[:, 3 * row : 3 * row + 3], jnp.zeros((1, 5), F32)], 1) for row in range(2)]
        spread_ratio = jnp.zeros(value.shape, F32)
        for index in range(5):
            inside = (where >= SMALL_EDGES[index]) & (where < SMALL_EDGES[index + 1])
            sums = []
            for slot, term in enumerate((value, direction)):
                square = jnp.where(inside, term * term, 0.0)
                sums.append(jnp.sum(jnp.sum(square, 1, keepdims=True), 0, keepdims=True))
                rows[slot] = jnp.where(lane == 3 + index, sums[slot], rows[slot])
            ratio = jnp.sqrt(sums[0]) / jnp.sqrt(sums[1] + UPDATE_EPS)
            spread_ratio = jnp.where(inside, ratio, spread_ratio)
        new = value - LEARN_RATE * spread_ratio * direction
        for index, result in enumerate((first_new, second_new, new)):
            for line in range(CONV_ROWS):
                tap, base = line // (CW // QB), line % (CW // QB) * QB
                outs[index][tap : tap + 1, base : base + QB] = result[line : line + 1]
            outs[3 + index][...] = result[CONV_ROWS:]
        outs[6][...] = jnp.sqrt(jnp.concatenate(rows, 0))

    outs = [jax.ShapeDtypeStruct(value.shape, F32) for value in (*params, *conv, *vec)]
    return whole_call(
        kernel, [squares, gathered, *params, *directions, *conv, *vec], outs + [jax.ShapeDtypeStruct((2, 8), F32)],
        "last_step",
    )


def adam_step(param, grad, first, second):
    first_new = FIRST_DECAY * first + (1.0 - FIRST_DECAY) * grad
    second_new = SECOND_DECAY * second + (1.0 - SECOND_DECAY) * grad * grad
    corrected = first_new / (1.0 - FIRST_DECAY**STEP)
    scaled = jnp.sqrt(second_new / (1.0 - SECOND_DECAY**STEP))
    return (first_new, second_new, corrected / (scaled + ADAM_EPS) + WEIGHT_DECAY * param)


def pad_row(values, width):
    return jnp.pad(values, (0, width - values.shape[0]))[None]


def eight_rows(values):
    return jnp.pad(values[None], ((0, 7), (0, 0)))


def hop(value, axis, distance):
    count = lax.axis_size(axis)
    return lax.ppermute(value, axis, [(index, index ^ distance) for index in range(count)])


def chip_groups():
    count = lax.axis_size("tok")
    return [list(range(core, count, 2)) for core in range(2)]


def pair_groups():
    count = lax.axis_size("tok")
    return [[first, first + 1] for first in range(0, count, 2)]


def gather_whole(piece):
    along = lax.all_gather(piece, "tok", axis_index_groups=chip_groups())
    across = lax.all_gather(along, "seq")
    pieces = lax.all_gather(across, "tok", axis_index_groups=pair_groups())
    core, seq, chip, rows, cols = pieces.shape
    return pieces.transpose(1, 3, 2, 0, 4).reshape(seq * rows, chip * core * cols)


def sum_cores(pieces):
    core = lax.axis_index("tok") % 2
    other = lax.dynamic_index_in_dim(pieces, 1 - core, 0, keepdims=False)
    own = lax.dynamic_index_in_dim(pieces, core, 0, keepdims=False)
    return own + hop(other, "tok", 1)


def sum_seq(pieces):
    moved = lax.all_to_all(pieces.astype(BF16), "seq", split_axis=0, concat_axis=0, tiled=True)
    return jnp.sum(moved.astype(F32), 0)


def sum_chips(pieces):
    moved = lax.all_to_all(
        pieces.astype(BF16), "tok", split_axis=0, concat_axis=0, axis_index_groups=chip_groups(), tiled=True
    )
    return jnp.sum(moved.astype(F32), 0)


class AnySlice:
    def __init__(self, w_zx, w_bc, w_out, length):
        self.seqs, self.toks = lax.axis_size("seq"), lax.axis_size("tok")
        zero = jnp.zeros((), jnp.int32)
        self.scalars = jnp.stack([zero, zero, zero, length])

    def begin(self, hidden_in, w_zx, w_bc, w_out):
        zx = gather_whole(w_zx.astype(BF16)).reshape(SEQS, ROWS_ZX, 2, 2, 2, TILE).transpose(2, 4, 0, 3, 1, 5)
        zx = zx.reshape(2, 2 * SEQS, 2 * ROWS_ZX, TILE)
        small = gather_whole(w_bc.astype(BF16)).reshape(SEQS, ROWS_ZX, CHIPS, 2, BC_EACH).transpose(3, 0, 2, 4, 1)
        small = jnp.pad(small, ((0, 0),) * 3 + ((0, ROWS_BC - BC_EACH), (0, 0)))
        small = small.reshape(2 * SEQS, CHIPS // 2, 2, ROWS_BC, ROWS_ZX).transpose(0, 1, 3, 2, 4)
        small = small.reshape(2 * SEQS, CHIPS // 2 * ROWS_BC, TILE)
        out = gather_whole(w_out.astype(BF16)).reshape(SEQS, TILE, CHIPS, 2, ROWS_OUT).transpose(3, 0, 2, 4, 1)
        self.rest = tuple(jnp.concatenate([zx[0], out.reshape(2 * SEQS, CHIPS * ROWS_OUT, TILE)], 1))
        return hidden_in, tuple(jnp.concatenate([zx[1], small], 1))

    def before_forward(self, *values):
        return values

    def after_forward(self, *values):
        return (*values, self.rest)

    def before_backward(self, normed, normed_t, gate_grad, branch_t, gated_low, *values):
        self.gate_grad = dot_tn(normed, gate_grad)
        self.out_grad = dot(branch_t, gated_low).T
        return values

    def after_backward(self, *values):
        return values

    def cut(self, array):
        rows, cols = array.shape
        shape = (self.seqs, rows // self.seqs, self.toks // 2, 2, cols // self.toks)
        return array.reshape(shape).transpose(3, 0, 2, 1, 4)

    def finish(self, normed, normed_t, pre_grad, other_grad, back, send, hidden_out, smalls):
        hidden_grad, gain_in_grad = back(pre_grad, ())
        columns = jnp.concatenate([self.gate_grad, dot_tn(normed, pre_grad[:, :XW])], 1)
        small = dot_tn(normed, pre_grad[:, XW:])[:, :BC_COLS]
        columns, small, out = (sum_chips(sum_seq(sum_cores(self.cut(value)))) for value in (columns, small, self.out_grad))
        width = columns.shape[1]
        small, out = (jnp.pad(value.T, ((0, 0), (0, width - value.shape[0]))) for value in (small, out))
        taps_grad, gain_out_grad, ssm_grad = smalls
        vector = jnp.concatenate(
            [taps_grad[:K].reshape(-1), gain_in_grad[0], gain_out_grad[0], taps_grad[K], ssm_grad[2]]
        )
        for axis in ("tok", "seq"):
            distance = 1
            while distance < lax.axis_size(axis):
                vector = vector + hop(vector, axis, distance)
                distance *= 2
        vector = jnp.pad(vector, (0, SMALL_ROWS * QB - vector.shape[0])).reshape(-1, 1, TILE)
        self.vector = jnp.pad(vector, ((0, 0), (0, 0), (QB, TILE)))
        self.starts = (0, columns.shape[0], columns.shape[0] + small.shape[0])
        return (jnp.concatenate([columns, small, out], 0),), send(hidden_grad), hidden_out

    def chunks(self, gathered):
        return self.vector


class ThisSlice:
    def __init__(self, w_zx, w_bc, w_out, length):
        tok = lax.axis_index("tok")
        self.low = tok < 4
        self.scalars = jnp.stack([lax.axis_index("seq"), tok // 2, tok % 2, length]).astype(jnp.int32)

    def chips(self, value):
        return [value] + [hop(value, "tok", 2 * distance) for distance in range(1, CHIPS)]

    def seqs(self, value):
        return [value] + [hop(value, "seq", distance) for distance in range(1, SEQS)]

    def others(self, values):
        return [hop(value, "tok", 1) for value in values]

    def begin(self, hidden_in, w_zx, w_bc, w_out):
        small = jnp.pad(w_bc.astype(BF16).T, ((0, ROWS_BC - BC_EACH), (0, TILE - ROWS_ZX)))
        first = self.chips(jnp.concatenate([w_zx.astype(BF16), small], 0))
        inner = [jnp.where(self.low, first[2 + index], first[index])[:ROWS_ZX] for index in range(2)]
        halves_of = [value[ROWS_ZX : ROWS_ZX + ROWS_BC, :ROWS_ZX] for value in first]
        small = [jnp.concatenate(halves_of[index : index + 2], 1) for index in range(0, CHIPS, 2)]
        inner = jnp.concatenate(inner + small, 0)
        hidden_in, inner, first = lax.optimization_barrier((hidden_in, inner, first))
        inner = self.seqs(inner)
        inner, first, w_out = lax.optimization_barrier((inner, first, w_out))
        self.gate = [jnp.where(self.low, first[index], first[2 + index])[:ROWS_ZX] for index in range(2)]
        self.out = self.chips(w_out.astype(BF16).T)
        return hidden_in, inner + self.others(inner)

    def before_forward(self, *values):
        *values, out = lax.optimization_barrier((*values, self.out))
        self.rest = self.seqs(pack_rows(self.gate + out))
        return values

    def after_forward(self, *values):
        *values, rest = lax.optimization_barrier((*values, self.rest))
        return (*values, rest + self.others(rest))

    def before_backward(self, normed, normed_t, gate_grad, branch_t, gated_low, *values):
        early = early_grads(self.scalars, normed_t, gate_grad, branch_t, gated_low)
        early, values, normed_t = lax.optimization_barrier((tuple(early), values, normed_t))
        self.early = (early[0],) + tuple(hop(early[index], "seq", index) for index in range(1, SEQS))
        self.sibling_t = hop(normed_t, "tok", 1)
        return values

    def after_backward(self, *values):
        values, self.early, self.sibling_t = lax.optimization_barrier((values, self.early, self.sibling_t))
        return values

    def total(self, parts):
        return sum(part.astype(F32) for part in parts)

    def by_seq(self, pieces):
        return [pieces[0]] + [hop(pieces[index], "seq", index) for index in range(1, SEQS)]

    def by_chips(self, pieces):
        return [pieces[0]] + [hop(pieces[index], "tok", 2 * index) for index in range(1, CHIPS)]

    def tree(self, parts):
        return (parts[0] + parts[1]) + (parts[2] + parts[3])

    def finish(self, normed, normed_t, pre_grad, other_grad, back, send, hidden_out, smalls):
        sibling_grad = hop(other_grad, "tok", 1)
        hidden_grad, gain_in_grad, rest, other_rest = back(pre_grad, self.early)
        hidden_grad, rest, other_rest, pre_grad, sibling_grad = lax.optimization_barrier(
            (hidden_grad, rest, other_rest, pre_grad, sibling_grad)
        )
        hidden_grad = send(hidden_grad)
        taps_grad, gain_out_grad, ssm_grad = smalls
        rest_arrived = hop(other_rest, "tok", 1)
        late = late_grads(
            self.scalars, normed_t, pre_grad, self.sibling_t, sibling_grad,
            (taps_grad, gain_in_grad, gain_out_grad, ssm_grad),
        )

        late, hidden_out, rest, rest_arrived = lax.optimization_barrier((late, hidden_out, rest, rest_arrived))
        late = self.by_seq(late)
        hidden_out = settle(hidden_out, "settle_out")
        late, hidden_out = lax.optimization_barrier((late, hidden_out))
        joint = chip_pieces(self.scalars, late, rest, rest_arrived)

        joint, hidden_grad = lax.optimization_barrier((joint, hidden_grad))
        hidden_grad = settle(hidden_grad, "settle_grad")
        joint = self.by_chips(joint)
        joint, hidden_grad = lax.optimization_barrier((joint, hidden_grad))
        self.starts = (0, ROWS_ZX, ROWS_ZX + ROWS_BC)
        return joint, hidden_grad, hidden_out

    def chunks(self, gathered):
        return gathered


def per_device(
    hidden_in, out_grad, lengths, w_zx, m_zx, v_zx, w_bc, m_bc, v_bc, w_out, m_out, v_out,
    conv_w, m_conv, v_conv, vectors, m_vec, v_vec,
):
    toks = lax.axis_size("tok")
    seq_group, local_len, _ = hidden_in.shape
    assert seq_group == toks
    total = seq_group * local_len

    def to_sequence(value):
        return lax.all_to_all(value, "tok", split_axis=0, concat_axis=0, tiled=True).reshape(total, D)

    def to_positions(value):
        return lax.all_to_all(
            value.reshape(seq_group, local_len, D), "tok", split_axis=0, concat_axis=0, tiled=True
        )

    length = lax.dynamic_index_in_dim(lengths, lax.axis_index("tok"), 0, keepdims=False)
    weights = (ThisSlice if (lax.axis_size("seq"), toks) == (4, 8) else AnySlice)(w_zx, w_bc, w_out, length)
    hidden_in, pieces = weights.begin(hidden_in, w_zx, w_bc, w_out)
    hidden = to_sequence(hidden_in)

    gain_in = eight_rows(vectors[:D])
    gain_out = eight_rows(vectors[D : D + E])
    conv_bias = vectors[D + E : D + E + CW]
    ssm_params = vectors[D + E + CW :]
    delta_bias, decay_log, skip_gain = ssm_params[: 2 * H], ssm_params[2 * H : 4 * H], ssm_params[4 * H :]
    taps = jnp.pad(jnp.concatenate([conv_w, conv_bias[None]], 0), ((0, 3), (0, 0)))
    ssm = jnp.pad(jnp.concatenate([pad_row(delta_bias, QB), pad_row(jnp.exp(decay_log), QB)], 0), ((0, 6), (0, 0)))
    skip = eight_rows(jnp.repeat(skip_gain, P_SIZE))

    inner_weights, small_weights = join_weights(weights.scalars, pieces)
    normed, normed_t, pre = project(hidden, gain_in, inner_weights, small_weights)
    pre, out_grad = weights.before_forward(pre, out_grad)
    upstream = to_sequence(out_grad)
    conv_low, mixed, run, delta, ahead, behind, slope = scan_forward(weights.scalars, pre, taps, ssm, skip)
    mixed, upstream, rest = weights.after_forward(mixed, upstream)

    hidden_out, gated_low, mixed_grad, gate_grad, branch_t, gain_out_grad, gate_weights = gated_norm(
        weights.scalars, normed, mixed, hidden, upstream, gain_out, rest
    )
    mixed_grad, hidden_out = weights.before_backward(
        normed, normed_t, gate_grad, branch_t, gated_low, mixed_grad, hidden_out
    )
    hidden_out = to_positions(hidden_out)

    pre_grad, other_grad, taps_grad, ssm_grad, skip_grad = scan_backward(
        weights.scalars, mixed_grad, conv_low, pre, slope, run, delta, ahead, behind, taps, ssm, skip
    )
    pre_grad, other_grad, hidden_out = weights.after_backward(pre_grad, other_grad, hidden_out)

    def back(pre_grad, early):
        return input_grad(
            gate_grad, pre_grad, hidden, upstream, gain_in, inner_weights, small_weights, gate_weights, early
        )

    parts, hidden_grad, hidden_out = weights.finish(
        normed, normed_t, pre_grad, other_grad, back, to_positions, hidden_out, (taps_grad, gain_out_grad, ssm_grad)
    )
    devices = lax.axis_size("seq") * toks
    w_bc_t, w_out_t = w_bc.T, w_out.T
    *stepped, squares = matrices_step(
        parts, weights.starts, (w_zx, m_zx, v_zx), (w_bc_t, m_bc.T, v_bc.T), (w_out_t, m_out.T, v_out.T), devices
    )
    squares = lax.all_to_all(squares, ("seq", "tok"), split_axis=0, concat_axis=0, tiled=True)

    def vector_rows(vector):
        return jnp.pad(vector, (0, (SMALL_ROWS - CONV_ROWS) * QB - vector.shape[0])).reshape(-1, QB)

    zx_new, bc_new, out_new, conv_first, conv_second, conv_new, *small_new, norms = last_step(
        squares, weights.chunks(squares), (w_zx, w_bc_t, w_out_t), stepped[2::3], (conv_w, m_conv, v_conv),
        tuple(vector_rows(value) for value in (vectors, m_vec, v_vec)),
    )
    vec_first, vec_second, vectors_new = (value.reshape(-1)[: vectors.shape[0]] for value in small_new)
    return (
        hidden_out,
        hidden_grad,
        stepped[0],
        stepped[1],
        zx_new,
        stepped[3].T,
        stepped[4].T,
        bc_new.T,
        stepped[6].T,
        stepped[7].T,
        out_new.T,
        conv_first,
        conv_second,
        conv_new,
        vec_first,
        vec_second,
        vectors_new,
        norms,
    )


def solution(mesh):
    placed = (
        P("seq", "tok", None),
        P("seq", "tok", None),
        P("seq"),
        P("seq", "tok"),
        P("seq", "tok"),
        P("seq", "tok"),
        P("seq", "tok"),
        P("seq", "tok"),
        P("seq", "tok"),
        P("seq", "tok"),
        P("seq", "tok"),
        P("seq", "tok"),
        P(),
        P(),
        P(),
        P(),
        P(),
        P(),
    )
    return jax.shard_map(
        per_device,
        mesh=mesh,
        in_specs=placed,
        out_specs=(
            P("seq", "tok", None),
            P("seq", "tok", None),
            P("seq", "tok"),
            P("seq", "tok"),
            P("seq", "tok"),
            P("seq", "tok"),
            P("seq", "tok"),
            P("seq", "tok"),
            P("seq", "tok"),
            P("seq", "tok"),
            P("seq", "tok"),
            P(),
            P(),
            P(),
            P(),
            P(),
            P(),
            P(),
        ),
        check_vma=False,
    )
```

time: 2680 us -> 340 us (0.13); the launches traced: 2640 us -> 339 us
  local copies, waits for them, and re-layouts: 1170 us -> 13.3 us
  matrix products: 478 us -> 0 us
  other arithmetic: 347 us -> 5.17 us
  waiting for transfers between devices: 406 us -> 73.3 us
  Pallas kernels: 0 us -> 191 us
  blocking collectives: 180 us -> 0 us
    dynamic_update_slice x68 -> x0, local copies, waits for them, and re-layouts: 722 us -> none  [the longest x64 721 us: stretch_scan(): lax.scan(jax.checkpoint(advance), initial, pieces, reverse=backward)]
    dot_general x233 -> x0, matrix products: 478 us -> none  [the longest x48 193 us: advance(): within = jnp.einsum('gijh,gjhp->gihp', weights, block_in, precision=HIGHEST)]
    all_to_all x6 -> x5, waiting for transfers between devices: 252 us -> 15 us  [the longest x2 7.61 us: to_sequence(): lax.all_to_all(value, 'tok', split_axis=0, concat_axis=0, tiled=True)]
    pallas_call x0 -> x14, Pallas kernels: none -> 191 us  [the longest x1 65.6 us: scan_backward(): pl.pallas_call(scan_backward_kernel, grid=(2 * blocks,), in_specs=[pl.Blo...]
    all_gather x3 -> x0, blocking collectives: 110 us -> none  [the longest x1 80.8 us: per_device(): lax.all_gather(w_out.astype(jnp.bfloat16), 'tok', axis=1, tiled=True)]
    another operation x69 -> x1, other arithmetic: 80.9 us -> 1.23 us  [__init__(): jnp.stack([lax.axis_index('seq'), tok // 2, tok % 2, length])]
    reduce_sum x51 -> x0, other arithmetic: 79.2 us -> none  [the longest x16 23.9 us: advance(): to_edge = jnp.exp(edge_sum[:, None, :] - running)]
    all_gather x3 -> x0, waiting for transfers between devices: 70.7 us -> none  [the longest x1 26.9 us: per_device(): lax.all_gather(w_zx.astype(jnp.bfloat16), 'tok', axis=1, tiled=True)]
  transfers between devices with their start and end apart: 17 -> 37, of which waited for: 12 -> 15; matrix products, arithmetic and copies ran while one was open for 8% -> 2% of each run, Pallas kernels for 0% -> 45%
where the time goes in v1:
time: 340 us; the launch traced here: 339 us
  Pallas kernels  191 us (56%)
  waiting for transfers between devices  73.3 us (22%)
  starting transfers between devices  54.8 us (16%)
  local copies, waits for them, and re-layouts  13.3 us (4%)
  other arithmetic  5.17 us (2%)
    pallas_call x1, Pallas kernels, scan_backward(): pl.pallas_call(scan_backward_kernel, grid=(2 * blocks,), in_specs=[pl.Blo...  65.6 us
    ppermute x32, waiting for transfers between devices, hop(): lax.ppermute(value, axis, [(index, index ^ distance) for index in range(c...  58.3 us
    pallas_call x5, Pallas kernels, scalar_call(): pl.pallas_call(kernel, grid_spec=spec, out_shape=outs, compiler_params=pl...  54.2 us
    pallas_call x1, Pallas kernels, scan_forward(): pl.pallas_call(scan_forward_kernel, grid=(2 * blocks,), in_specs=[pl.Bloc...  36.5 us
    ppermute x32, starting transfers between devices, hop(): lax.ppermute(value, axis, [(index, index ^ distance) for index in range(c...  31.8 us
    pallas_call x1, Pallas kernels, input_grad(): pl.pallas_call(kernel, grid=(steps,), in_specs=[rows(E), rows(PW), rows(D...  12.6 us
    unnamed x76, local copies, waits for them, and re-layouts  9.29 us
    all_to_all x2, starting transfers between devices, to_positions(): lax.all_to_all(value.reshape(seq_group, local_len, D), 'tok', split_axis=...  9.2 us
  transfers between devices with their start and end apart: 37, of which 15 were waited for; matrix products, arithmetic and copies ran while one was open for 2% of the time, Pallas kernels for 45%

profile of v1, /device:TPU:0, one launch (start us, length us, event | category | flops | bytes accessed | tf_op | source)
XLA Modules:
  0.0 339.3 jit_solution(6867563041639688813)
XLA Ops:
  2.5 5.1 %collective-permute-start.1 = (bf16[240,384]{1,0:T(8,128)(2,1)S(1)}, bf16[240,384]{1,0:T(8,128)(2,1)S(1)}, u32[]{:S(2)}, u32[]{:S(2)}) collective-permute-start(bf16[240,384]{1,0:T(8,128)(2,1)S(1)} %pad_maximum_fusion), channel_id=1, source_target_pairs={{0,6},{1,7},{2,4},{3,5},{4,2},{5,3},{6,0},{7,1},{8,14},{9,15},{10,... | collective-permute-start | bytes 552968 | tf_op jit(solution)/shard_map/ppermute | solution.py:1152
  8.2 4.9 %collective-permute-done.1 = bf16[240,384]{1,0:T(8,128)(2,1)S(1)} collective-permute-done((bf16[240,384]{1,0:T(8,128)(2,1)S(1)}, bf16[240,384]{1,0:T(8,128)(2,1)S(1)}, u32[]{:S(2)}, u32[]{:S(2)}) %collective-permute-start.1) | collective-permute-done | bytes 184352 | tf_op jit(solution)/shard_map/ppermute | solution.py:1152
  13.2 10.0 %collective-permute-done = bf16[240,384]{1,0:T(8,128)(2,1)S(1)} collective-permute-done((bf16[240,384]{1,0:T(8,128)(2,1)S(1)}, bf16[240,384]{1,0:T(8,128)(2,1)S(1)}, u32[]{:S(2)}, u32[]{:S(2)}) %collective-permute-start) | collective-permute-done | bytes 184352 | tf_op jit(solution)/shard_map/ppermute | solution.py:1152
  23.5 3.9 %all-to-all-start = ((bf16[8,128,768]{2,1,0:T(8,128)(2,1)}), bf16[8,128,768]{2,1,0:T(8,128)(2,1)S(1)}, u32[]{:S(2)}, u32[]{:S(2)}) async-start(bf16[8,128,768]{2,1,0:T(8,128)(2,1)} %param.25), calls=%async_computation | async-start | bytes 3145728 | tf_op jit(solution)/shard_map/all_to_all | solution.py:1355
  35.5 3.9 %collective-permute-done.3.refs_1_ = bf16[480,384]{1,0:T(8,128)(2,1)S(1)} collective-permute-done((bf16[480,384]{1,0:T(8,128)(2,1)S(1)}, bf16[480,384]{1,0:T(8,128)(2,1)S(1)}, u32[]{:S(2)}, u32[]{:S(2)}) %collective-permute-start.3) | collective-permute-done | bytes 368672 | tf_op jit(solution)/shard_map/ppermute | solution.py:1152
  39.4 8.8 %collective-permute-done.4.refs_2_ = bf16[480,384]{1,0:T(8,128)(2,1)} collective-permute-done((bf16[480,384]{1,0:T(8,128)(2,1)S(1)}, bf16[480,384]{1,0:T(8,128)(2,1)}, u32[]{:S(2)}, u32[]{:S(2)}) %collective-permute-start.4) | collective-permute-done | bytes 368672 | tf_op jit(solution)/shard_map/ppermute | solution.py:1152
  51.8 2.4 collective-permute-start.11
  56.1 6.1 %join_weights.1 = (bf16[768,1536]{1,0:T(8,128)(2,1)}, bf16[384,768]{1,0:T(8,128)(2,1)}) custom-call(s32[4]{0:T(128)} %pad_add_fusion.place.place_ref, bf16[384,384]{1,0:T(8,128)(2,1)} %constant.52.clone.row_ref, bf16[1024,768]{1,0:T(8,128)(2,1)} %constant.53.clone.col_ref, bf16[480,384]{1,0:T(8,128)(2,1)} %copy-done.6, bf16[480,384]{1,0:T(8,128)(2,1)} %copy-done.13, ...), custom_call_target="tpu_custom_call" | custom-call | flops 1 | bytes 1 | tf_op jit(solution)/shard_map/join_weights/pallas_call | solution.py:627
  62.2 6.6 %all-to-all-done = bf16[8,128,768]{2,1,0:T(8,128)(2,1)S(1)} async-done(((bf16[8,128,768]{2,1,0:T(8,128)(2,1)}), bf16[8,128,768]{2,1,0:T(8,128)(2,1)S(1)}, u32[]{:S(2)}, u32[]{:S(2)}) %all-to-all-start) | async-done | bytes 1572896 | tf_op jit(solution)/shard_map/all_to_all | solution.py:1355
  70.0 7.6 %project.1 = (bf16[1024,768]{1,0:T(8,128)(2,1)}, bf16[768,1024]{1,0:T(8,128)(2,1)}, bf16[1024,1920]{1,0:T(8,128)(2,1)}) custom-call(bf16[1024,768]{1,0:T(8,128)(2,1)} %bitcast.39, f32[8,768]{1,0:T(8,128)} %pad.41.gain_ref, bf16[768,1536]{1,0:T(8,128)(2,1)} %get-tuple-element.156.wide_ref.inner_w, bf16[384,768]{1,0:T(8,128)(2,1)} %get-tuple-element.157.small_ref.small_w), custom_call_target="tpu_custom_call" | custom-call | flops 12079595520 | bytes 1 | tf_op jit(solution)/shard_map/project/pallas_call | solution.py:713
  78.3 2.0 pack_rows.1.refs_0_
  83.8 3.8 %all-to-all-start.1 = ((bf16[8,128,768]{2,1,0:T(8,128)(2,1)}), bf16[8,128,768]{2,1,0:T(8,128)(2,1)S(1)}, u32[]{:S(2)}, u32[]{:S(2)}) async-start(bf16[8,128,768]{2,1,0:T(8,128)(2,1)} %param.26), calls=%async_computation.1 | async-start | bytes 3145728 | tf_op jit(solution)/shard_map/all_to_all | solution.py:1355
  87.6 36.5 %scan_forward.1 = (bf16[1024,1792]{1,0:T(8,128)(2,1)}, bf16[1024,1536]{1,0:T(8,128)(2,1)}, f32[1024,128]{1,0:T(8,128)}, f32[1024,128]{1,0:T(8,128)}, bf16[1024,1...) custom-call(s32[4]{0:T(128)} %pad_add_fusion.place.place_ref, ...), custom_call_target="tpu_custom_call" | custom-call | flops 40894464000 | bytes 1 | tf_op jit(solution)/shard_map/scan_forward/pallas_call | solution.py:491
  130.7 20.1 %gated_norm.1 = (bf16[1024,768]{1,0:T(8,128)(2,1)}, bf16[1024,1536]{1,0:T(8,128)(2,1)}, bf16[1024,1536]{1,0:T(8,128)(2,1)}, bf16[1024,1536]{1,0:T(8,128)(2,1)}, ...) custom-call(s32[4]{0:T(128)} %pad_add_fusion.place.place_ref, ...), custom_call_target="tpu_custom_call" | custom-call | flops 22951231488 | bytes 1 | tf_op jit(solution)/shard_map/gated_norm/pallas_call | solution.py:627
  150.9 11.9 %early_grads.1 = (bf16[2,768,384]{2,1,0:T(8,128)(2,1)}, bf16[2,768,384]{2,1,0:T(8,128)(2,1)}, bf16[2,768,384]{2,1,0:T(8,128)(2,1)}, bf16[2,768,384]{2,1,0:T(8,128)(2,1)}) custom-call(s32[4]{0:T(128)} %pad_add_fusion.place.place_ref, bf16[768,1024]{1,0:T(8,128)(2,1)} %get-tuple-element.202.normed_ref.own_t_ref, ...), custom_call_target="tpu_custom_call" | custom-call | flops 1 | bytes 1 | tf_op jit(solution)/shard_map/early_grads/pallas_call | solution.py:627
  162.8 4.1 %all-to-all-start.2 = ((bf16[8,128,768]{2,1,0:T(8,128)(2,1)}), bf16[8,128,768]{2,1,0:T(8,128)(2,1)S(1)}, u32[]{:S(2)}, u32[]{:S(2)}) async-start(bf16[8,128,768]{2,1,0:T(8,128)(2,1)} %bitcast.45), calls=%async_computation.2 | async-start | bytes 3145728 | tf_op jit(solution)/shard_map/all_to_all | solution.py:1358
  170.3 65.6 %scan_backward.1 = (bf16[1024,1920]{1,0:T(8,128)(2,1)}, bf16[1024,1152]{1,0:T(8,128)(2,1)}, f32[8,1792]{1,0:T(8,128)}, f32[8,128]{1,0:T(8,128)}, f32[8,1536]{1,0:T(8,128)}) custom-call(s32[4]{0:T(128)} %pad_add_fusion.place.place_ref, bf16[1024,1536]{1,0:T(8,128)(2,1)} %get-tuple-element.188.grad_ref, bf16[1024,1792]{1,0:T(8,128)(2,1)} %get-tuple-element.189.conv_ref, ...), custom_call_target="tpu_custom_call" | custom-call | flops 75497472000 | bytes 1 | tf_op jit(solution)/shard_map/scan_backward/pallas_call | solution.py:547
  237.9 12.6 %input_grad.1 = (bf16[1024,768]{1,0:T(8,128)(2,1)}, f32[8,768]{1,0:T(8,128)}, f32[768,384]{1,0:T(8,128)}, f32[768,384]{1,0:T(8,128)}) custom-call(bf16[1024,1536]{1,0:T(8,128)(2,1)} %get-tuple-element.179.gate_ref, bf16[1024,1920]{1,0:T(8,128)(2,1)} %get-tuple-element.214.pre_ref.grad_ref, bf16[1024,768]{1,0:T(8,128)(2,1)} %bitcast.41, ...), custom_call_target="tpu_custom_call" | custom-call | flops 1 | bytes 1 | tf_op jit(solution)/shard_map/input_grad/pallas_call | solution.py:824
  252.0 5.1 %all-to-all-start.3 = ((bf16[8,128,768]{2,1,0:T(8,128)(2,1)}), bf16[8,128,768]{2,1,0:T(8,128)(2,1)S(1)}, u32[]{:S(2)}, u32[]{:S(2)}) async-start(bf16[8,128,768]{2,1,0:T(8,128)(2,1)} %bitcast.44), calls=%async_computation.3 | async-start | bytes 3145728 | tf_op jit(solution)/shard_map/all_to_all | solution.py:1358
  257.6 11.8 %late_grads.1 = (bf16[480,384]{1,0:T(8,128)(2,1)}, bf16[480,384]{1,0:T(8,128)(2,1)}, bf16[480,384]{1,0:T(8,128)(2,1)}, bf16[480,384]{1,0:T(8,128)(2,1)}) custom-call(s32[4]{0:T(128)} %pad_add_fusion.place.place_ref, bf16[768,1024]{1,0:T(8,128)(2,1)} %get-tuple-element.202.normed_ref.own_t_ref, bf16[768,1024]{1,0:T(8,128)(2,1)} %collective-permute-done.23.other_t_ref, ...), custom_call_target="tpu_custom_call" | custom-call | flops 1 | bytes 1 | tf_op jit(solution)/shard_map/late_grads/pallas_call | solution.py:627
  273.0 3.6 %settle_out.1 = bf16[8,128,768]{2,1,0:T(8,128)(2,1)} custom-call(bf16[8,128,768]{2,1,0:T(8,128)(2,1)} %copy-done), custom_call_target="tpu_custom_call" | custom-call | tf_op jit(solution)/shard_map/settle_out/pallas_call | solution.py:1075
  276.6 4.6 %collective-permute-done.26.refs_1_ = bf16[480,384]{1,0:T(8,128)(2,1)S(1)} collective-permute-done((bf16[480,384]{1,0:T(8,128)(2,1)}, bf16[480,384]{1,0:T(8,128)(2,1)S(1)}, u32[]{:S(2)}, u32[]{:S(2)}) %collective-permute-start.26) | collective-permute-done | bytes 368672 | tf_op jit(solution)/shard_map/ppermute | solution.py:1152
  281.2 8.2 %collective-permute-done.27.refs_2_ = bf16[480,384]{1,0:T(8,128)(2,1)S(1)} collective-permute-done((bf16[480,384]{1,0:T(8,128)(2,1)}, bf16[480,384]{1,0:T(8,128)(2,1)S(1)}, u32[]{:S(2)}, u32[]{:S(2)}) %collective-permute-start.27) | collective-permute-done | bytes 368672 | tf_op jit(solution)/shard_map/ppermute | solution.py:1152
  290.2 4.2 %chip_pieces.1 = (bf16[336,384]{1,0:T(8,128)(2,1)}, bf16[336,384]{1,0:T(8,128)(2,1)}, bf16[336,384]{1,0:T(8,128)(2,1)}, bf16[336,384]{1,0:T(8,128)(2,1)}) custom-call(s32[4]{0:T(128)} %pad_add_fusion.place.place_ref, bf16[480,384]{1,0:T(8,128)(2,1)} %get-tuple-element.233.refs_0_, bf16[480,384]{1,0:T(8,128)(2,1)} %copy-done.18, bf16[480,384]{1,0:T(8,128)(2,1)} %copy-done.19, ...), custom_call_target="tpu_custom_call" | custom-call | flops 1 | bytes 1 | tf_op jit(solution)/shard_map/chip_pieces/pallas_call | solution.py:627
  296.4 2.4 collective-permute-start.30
  299.3 3.6 %settle_grad.1 = bf16[8,128,768]{2,1,0:T(8,128)(2,1)} custom-call(bf16[8,128,768]{2,1,0:T(8,128)(2,1)} %copy-done.1), custom_call_target="tpu_custom_call" | custom-call | tf_op jit(solution)/shard_map/settle_grad/pallas_call | solution.py:1075
  302.9 4.2 %collective-permute-done.29.refs_1_ = bf16[336,384]{1,0:T(8,128)(2,1)S(1)} collective-permute-done((bf16[336,384]{1,0:T(8,128)(2,1)}, bf16[336,384]{1,0:T(8,128)(2,1)S(1)}, u32[]{:S(2)}, u32[]{:S(2)}) %collective-permute-start.29) | collective-permute-done | bytes 258080 | tf_op jit(solution)/shard_map/ppermute | solution.py:1152
  307.1 10.7 %collective-permute-done.30.refs_2_ = bf16[336,384]{1,0:T(8,128)(2,1)S(1)} collective-permute-done((bf16[336,384]{1,0:T(8,128)(2,1)}, bf16[336,384]{1,0:T(8,128)(2,1)S(1)}, u32[]{:S(2)}, u32[]{:S(2)}) %collective-permute-start.30) | collective-permute-done | bytes 258080 | tf_op jit(solution)/shard_map/ppermute | solution.py:1152
  318.5 3.3 matrices_step.1
  321.8 6.2 %all-to-all-start.4 = ((f32[32,1,896]{2,1,0:T(1,128)}), f32[32,1,896]{2,1,0:T(1,128)S(1)}, u32[]{:S(2)}, u32[]{:S(2)}) async-start(f32[32,1,896]{2,1,0:T(1,128)} %get-tuple-element.256), calls=%async_computation.4 | async-start | bytes 229376 | tf_op jit(solution)/shard_map/all_to_all | solution.py:1409
  329.2 6.8 %all-to-all-done.4.squares_ref.gathered_ref = f32[32,1,896]{2,1,0:T(1,128)S(1)} async-done(((f32[32,1,896]{2,1,0:T(1,128)}), f32[32,1,896]{2,1,0:T(1,128)S(1)}, u32[]{:S(2)}, u32[]{:S(2)}) %all-to-all-start.4) | async-done | bytes 114720 | tf_op jit(solution)/shard_map/all_to_all | solution.py:1409
  336.6 2.4 last_step.1
  (166 shorter events, 45.0 us)
Async XLA Ops:
  2.5 10.7 %collective-permute-start.1 = (bf16[240,384]{1,0:T(8,128)(2,1)S(1)}, bf16[240,384]{1,0:T(8,128)(2,1)S(1)}, u32[]{:S(2)}, u32[]{:S(2)}) collective-permute-start(bf16[240,384]{1,0:T(8,128)(2,1)S(1)} %pad_maximum_fusion), channel_id=1, source_target_pairs={{0,6},{1,7},{2,4},{3,5},{4,2},{5,3},{6,0},{7,1},{8,14},{9,15},{10,... | collective-permute-start | bytes 552968 | tf_op jit(solution)/shard_map/ppermute | solution.py:1152
  7.6 15.6 %collective-permute-start = (bf16[240,384]{1,0:T(8,128)(2,1)S(1)}, bf16[240,384]{1,0:T(8,128)(2,1)S(1)}, u32[]{:S(2)}, u32[]{:S(2)}) collective-permute-start(bf16[240,384]{1,0:T(8,128)(2,1)S(1)} %pad_maximum_fusion), channel_id=1, source_target_pairs={{0,4},{1,5},{2,6},{3,7},{4,0},{5,1},{6,2},{7,3},{8,12},{9,13},{10,... | collective-permute-start | bytes 552968 | tf_op jit(solution)/shard_map/ppermute | solution.py:1152
  7.6 15.6 %collective-permute-start.2 = (bf16[240,384]{1,0:T(8,128)(2,1)S(1)}, bf16[240,384]{1,0:T(8,128)(2,1)S(1)}, u32[]{:S(2)}, u32[]{:S(2)}) collective-permute-start(bf16[240,384]{1,0:T(8,128)(2,1)S(1)} %pad_maximum_fusion), channel_id=1, source_target_pairs={{0,2},{1,3},{2,0},{3,1},{4,6},{5,7},{6,4},{7,5},{8,10},{9,11},{10,... | collective-permute-start | bytes 552968 | tf_op jit(solution)/shard_map/ppermute | solution.py:1152
  23.5 45.4 %all-to-all-start = ((bf16[8,128,768]{2,1,0:T(8,128)(2,1)}), bf16[8,128,768]{2,1,0:T(8,128)(2,1)S(1)}, u32[]{:S(2)}, u32[]{:S(2)}) async-start(bf16[8,128,768]{2,1,0:T(8,128)(2,1)} %param.25), calls=%async_computation | async-start | bytes 3145728 | tf_op jit(solution)/shard_map/all_to_all | solution.py:1355
  28.0 11.4 %collective-permute-start.3 = (bf16[480,384]{1,0:T(8,128)(2,1)S(1)}, bf16[480,384]{1,0:T(8,128)(2,1)S(1)}, u32[]{:S(2)}, u32[]{:S(2)}) collective-permute-start(bf16[480,384]{1,0:T(8,128)(2,1)S(1)} %maximum_maximum_fusion.refs_0_), channel_id=1, source_target_pairs={{0,8},{8,0},{16,24},{24,16},{1,9},{9,1},{17,25},{25,17},{2,10},{10... | collective-permute-start | bytes 1105928 | tf_op jit(solution)/shard_map/ppermute | solution.py:1152
  29.5 18.7 %collective-permute-start.4 = (bf16[480,384]{1,0:T(8,128)(2,1)S(1)}, bf16[480,384]{1,0:T(8,128)(2,1)}, u32[]{:S(2)}, u32[]{:S(2)}) collective-permute-start(bf16[480,384]{1,0:T(8,128)(2,1)S(1)} %maximum_maximum_fusion.refs_0_), channel_id=1, source_target_pairs={{0,16},{8,24},{16,0},{24,8},{1,17},{9,25},{17,1},{25,9},{2,18},{10... | collective-permute-start | bytes 1105928 | tf_op jit(solution)/shard_map/ppermute | solution.py:1152
  31.1 17.2 %collective-permute-start.5 = (bf16[480,384]{1,0:T(8,128)(2,1)S(1)}, bf16[480,384]{1,0:T(8,128)(2,1)}, u32[]{:S(2)}, u32[]{:S(2)}) collective-permute-start(bf16[480,384]{1,0:T(8,128)(2,1)S(1)} %maximum_maximum_fusion.refs_0_), channel_id=1, source_target_pairs={{0,24},{8,16},{16,8},{24,0},{1,25},{9,17},{17,9},{25,1},{2,26},{10... | collective-permute-start | bytes 1105928 | tf_op jit(solution)/shard_map/ppermute | solution.py:1152
  48.3 5.9 %collective-permute-start.7 = (bf16[480,384]{1,0:T(8,128)(2,1)S(1)}, bf16[480,384]{1,0:T(8,128)(2,1)S(1)}, u32[]{:S(2)}, u32[]{:S(2)}) collective-permute-start(bf16[480,384]{1,0:T(8,128)(2,1)S(1)} %collective-permute-done.3.refs_1_), channel_id=1, source_target_pairs={{0,1},{1,0},{2,3},{3,2},{4,5},{5,4},{6,7},{7,6},{8,9},{9,8},{10,11... | collective-permute-start | bytes 1105928 | tf_op jit(solution)/shard_map/ppermute | solution.py:1152
  48.8 5.8 %collective-permute-start.8 = (bf16[480,384]{1,0:T(8,128)(2,1)}, bf16[480,384]{1,0:T(8,128)(2,1)S(1)}, u32[]{:S(2)}, u32[]{:S(2)}) collective-permute-start(bf16[480,384]{1,0:T(8,128)(2,1)} %collective-permute-done.4.refs_2_), channel_id=1, source_target_pairs={{0,1},{1,0},{2,3},{3,2},{4,5},{5,4},{6,7},{7,6},{8,9},{9,8},{10,11... | collective-permute-start | bytes 1105928 | tf_op jit(solution)/shard_map/ppermute | solution.py:1152
  48.9 5.7 %collective-permute-start.9 = (bf16[480,384]{1,0:T(8,128)(2,1)}, bf16[480,384]{1,0:T(8,128)(2,1)S(1)}, u32[]{:S(2)}, u32[]{:S(2)}) collective-permute-start(bf16[480,384]{1,0:T(8,128)(2,1)} %collective-permute-done.5.refs_3_), channel_id=1, source_target_pairs={{0,1},{1,0},{2,3},{3,2},{4,5},{5,4},{6,7},{7,6},{8,9},{9,8},{10,11... | collective-permute-start | bytes 1105928 | tf_op jit(solution)/shard_map/ppermute | solution.py:1152
  49.3 28.3 %collective-permute-start.10 = (bf16[96,384]{1,0:T(8,128)(2,1)S(1)}, bf16[96,384]{1,0:T(8,128)(2,1)S(1)}, u32[]{:S(2)}, u32[]{:S(2)}) collective-permute-start(bf16[96,384]{1,0:T(8,128)(2,1)S(1)} %convert_bitcast_fusion.refs_2_), channel_id=1, source_target_pairs={{0,2},{1,3},{2,0},{3,1},{4,6},{5,7},{6,4},{7,5},{8,10},{9,11},{10,... | collective-permute-start | bytes 221192 | tf_op jit(solution)/shard_map/ppermute | solution.py:1152
  51.8 25.8 %collective-permute-start.11 = (bf16[96,384]{1,0:T(8,128)(2,1)S(1)}, bf16[96,384]{1,0:T(8,128)(2,1)S(1)}, u32[]{:S(2)}, u32[]{:S(2)}) collective-permute-start(bf16[96,384]{1,0:T(8,128)(2,1)S(1)} %convert_bitcast_fusion.refs_2_), channel_id=1, source_target_pairs={{0,4},{1,5},{2,6},{3,7},{4,0},{5,1},{6,2},{7,3},{8,12},{9,13},{10,... | collective-permute-start | bytes 221192 | tf_op jit(solution)/shard_map/ppermute | solution.py:1152
  54.2 23.5 %collective-permute-start.12 = (bf16[96,384]{1,0:T(8,128)(2,1)S(1)}, bf16[96,384]{1,0:T(8,128)(2,1)S(1)}, u32[]{:S(2)}, u32[]{:S(2)}) collective-permute-start(bf16[96,384]{1,0:T(8,128)(2,1)S(1)} %convert_bitcast_fusion.refs_2_), channel_id=1, source_target_pairs={{0,6},{1,7},{2,4},{3,5},{4,2},{5,3},{6,0},{7,1},{8,14},{9,15},{10,... | collective-permute-start | bytes 221192 | tf_op jit(solution)/shard_map/ppermute | solution.py:1152
  80.3 43.8 %collective-permute-start.13 = (bf16[768,384]{1,0:T(8,128)(2,1)}, bf16[768,384]{1,0:T(8,128)(2,1)S(1)}, u32[]{:S(2)}, u32[]{:S(2)}) collective-permute-start(bf16[768,384]{1,0:T(8,128)(2,1)} %pack_rows.1.refs_0_), channel_id=1, source_target_pairs={{0,8},{8,0},{16,24},{24,16},{1,9},{9,1},{17,25},{25,17},{2,10},{10... | collective-permute-start | bytes 1769480 | tf_op jit(solution)/shard_map/ppermute | solution.py:1152
  81.8 42.3 %collective-permute-start.14 = (bf16[768,384]{1,0:T(8,128)(2,1)}, bf16[768,384]{1,0:T(8,128)(2,1)S(1)}, u32[]{:S(2)}, u32[]{:S(2)}) collective-permute-start(bf16[768,384]{1,0:T(8,128)(2,1)} %pack_rows.1.refs_0_), channel_id=1, source_target_pairs={{0,16},{8,24},{16,0},{24,8},{1,17},{9,25},{17,1},{25,9},{2,18},{10... | collective-permute-start | bytes 1769480 | tf_op jit(solution)/shard_map/ppermute | solution.py:1152
  83.3 40.8 %collective-permute-start.15 = (bf16[768,384]{1,0:T(8,128)(2,1)}, bf16[768,384]{1,0:T(8,128)(2,1)}, u32[]{:S(2)}, u32[]{:S(2)}) collective-permute-start(bf16[768,384]{1,0:T(8,128)(2,1)} %pack_rows.1.refs_0_), channel_id=1, source_target_pairs={{0,24},{8,16},{16,8},{24,0},{1,25},{9,17},{17,9},{25,1},{2,26},{10... | collective-permute-start | bytes 1769480 | tf_op jit(solution)/shard_map/ppermute | solution.py:1152
  83.8 41.3 %all-to-all-start.1 = ((bf16[8,128,768]{2,1,0:T(8,128)(2,1)}), bf16[8,128,768]{2,1,0:T(8,128)(2,1)S(1)}, u32[]{:S(2)}, u32[]{:S(2)}) async-start(bf16[8,128,768]{2,1,0:T(8,128)(2,1)} %param.26), calls=%async_computation.1 | async-start | bytes 3145728 | tf_op jit(solution)/shard_map/all_to_all | solution.py:1355
  162.8 74.6 %all-to-all-start.2 = ((bf16[8,128,768]{2,1,0:T(8,128)(2,1)}), bf16[8,128,768]{2,1,0:T(8,128)(2,1)S(1)}, u32[]{:S(2)}, u32[]{:S(2)}) async-start(bf16[8,128,768]{2,1,0:T(8,128)(2,1)} %bitcast.45), calls=%async_computation.2 | async-start | bytes 3145728 | tf_op jit(solution)/shard_map/all_to_all | solution.py:1358
  166.8 69.1 %collective-permute-start.20 = (bf16[2,768,384]{2,1,0:T(8,128)(2,1)}, bf16[2,768,384]{2,1,0:T(8,128)(2,1)S(1)}, u32[]{:S(2)}, u32[]{:S(2)}) collective-permute-start(bf16[2,768,384]{2,1,0:T(8,128)(2,1)} %get-tuple-element.199), channel_id=1, source_target_pairs={{0,8},{8,0},{16,24},{24,16},{1,9},{9,1},{17,25},{25,17},{2,10},{10... | collective-permute-start | bytes 3538952 | tf_op jit(solution)/shard_map/ppermute | solution.py:1152
  168.3 67.6 %collective-permute-start.21 = (bf16[2,768,384]{2,1,0:T(8,128)(2,1)}, bf16[2,768,384]{2,1,0:T(8,128)(2,1)S(1)}, u32[]{:S(2)}, u32[]{:S(2)}) collective-permute-start(bf16[2,768,384]{2,1,0:T(8,128)(2,1)} %get-tuple-element.200), channel_id=1, source_target_pairs={{0,16},{8,24},{16,0},{24,8},{1,17},{9,25},{17,1},{25,9},{2,18},{10... | collective-permute-start | bytes 3538952 | tf_op jit(solution)/shard_map/ppermute | solution.py:1152
  169.9 66.1 %collective-permute-start.22 = (bf16[2,768,384]{2,1,0:T(8,128)(2,1)}, bf16[2,768,384]{2,1,0:T(8,128)(2,1)}, u32[]{:S(2)}, u32[]{:S(2)}) collective-permute-start(bf16[2,768,384]{2,1,0:T(8,128)(2,1)} %get-tuple-element.201), channel_id=1, source_target_pairs={{0,24},{8,16},{16,8},{24,0},{1,25},{9,17},{17,9},{25,1},{2,26},{10... | collective-permute-start | bytes 3538952 | tf_op jit(solution)/shard_map/ppermute | solution.py:1152
  170.3 67.0 %collective-permute-start.23 = (bf16[768,1024]{1,0:T(8,128)(2,1)S(1)}, bf16[768,1024]{1,0:T(8,128)(2,1)}, u32[]{:S(2)}, u32[]{:S(2)}) collective-permute-start(bf16[768,1024]{1,0:T(8,128)(2,1)S(1)} %copy-done.2), channel_id=1, source_target_pairs={{0,1},{1,0},{2,3},{3,2},{4,5},{5,4},{6,7},{7,6},{8,9},{9,8},{10,11... | collective-permute-start | bytes 4718600 | tf_op jit(solution)/shard_map/ppermute | solution.py:1152
  237.3 13.2 %collective-permute-start.24 = (bf16[1024,1152]{1,0:T(8,128)(2,1)}, bf16[1024,1152]{1,0:T(8,128)(2,1)S(1)}, u32[]{:S(2)}, u32[]{:S(2)}) collective-permute-start(bf16[1024,1152]{1,0:T(8,128)(2,1)} %get-tuple-element.213), channel_id=1, source_target_pairs={{0,1},{1,0},{2,3},{3,2},{4,5},{5,4},{6,7},{7,6},{8,9},{9,8},{10,11... | collective-permute-start | bytes 7077896 | tf_op jit(solution)/shard_map/ppermute | solution.py:1152
  252.0 43.0 %all-to-all-start.3 = ((bf16[8,128,768]{2,1,0:T(8,128)(2,1)}), bf16[8,128,768]{2,1,0:T(8,128)(2,1)S(1)}, u32[]{:S(2)}, u32[]{:S(2)}) async-start(bf16[8,128,768]{2,1,0:T(8,128)(2,1)} %bitcast.44), calls=%async_computation.3 | async-start | bytes 3145728 | tf_op jit(solution)/shard_map/all_to_all | solution.py:1358
  257.1 12.4 %collective-permute-start.25 = (f32[768,384]{1,0:T(8,128)}, f32[768,384]{1,0:T(8,128)S(1)}, u32[]{:S(2)}, u32[]{:S(2)}) collective-permute-start(f32[768,384]{1,0:T(8,128)} %get-tuple-element.226), channel_id=1, source_target_pairs={{0,1},{1,0},{2,3},{3,2},{4,5},{5,4},{6,7},{7,6},{8,9},{9,8},{10,11... | collective-permute-start | bytes 3538952 | tf_op jit(solution)/shard_map/ppermute | solution.py:1152
  269.5 11.7 %collective-permute-start.26 = (bf16[480,384]{1,0:T(8,128)(2,1)}, bf16[480,384]{1,0:T(8,128)(2,1)S(1)}, u32[]{:S(2)}, u32[]{:S(2)}) collective-permute-start(bf16[480,384]{1,0:T(8,128)(2,1)} %get-tuple-element.228), channel_id=1, source_target_pairs={{0,8},{8,0},{16,24},{24,16},{1,9},{9,1},{17,25},{25,17},{2,10},{10... | collective-permute-start | bytes 1105928 | tf_op jit(solution)/shard_map/ppermute | solution.py:1152
  271.1 18.3 %collective-permute-start.27 = (bf16[480,384]{1,0:T(8,128)(2,1)}, bf16[480,384]{1,0:T(8,128)(2,1)S(1)}, u32[]{:S(2)}, u32[]{:S(2)}) collective-permute-start(bf16[480,384]{1,0:T(8,128)(2,1)} %get-tuple-element.229), channel_id=1, source_target_pairs={{0,16},{8,24},{16,0},{24,8},{1,17},{9,25},{17,1},{25,9},{2,18},{10... | collective-permute-start | bytes 1105928 | tf_op jit(solution)/shard_map/ppermute | solution.py:1152
  272.6 16.8 %collective-permute-start.28 = (bf16[480,384]{1,0:T(8,128)(2,1)}, bf16[480,384]{1,0:T(8,128)(2,1)}, u32[]{:S(2)}, u32[]{:S(2)}) collective-permute-start(bf16[480,384]{1,0:T(8,128)(2,1)} %get-tuple-element.230), channel_id=1, source_target_pairs={{0,24},{8,16},{16,8},{24,0},{1,25},{9,17},{17,9},{25,1},{2,26},{10... | collective-permute-start | bytes 1105928 | tf_op jit(solution)/shard_map/ppermute | solution.py:1152
  295.0 12.1 %collective-permute-start.29 = (bf16[336,384]{1,0:T(8,128)(2,1)}, bf16[336,384]{1,0:T(8,128)(2,1)S(1)}, u32[]{:S(2)}, u32[]{:S(2)}) collective-permute-start(bf16[336,384]{1,0:T(8,128)(2,1)} %get-tuple-element.245), channel_id=1, source_target_pairs={{0,2},{1,3},{2,0},{3,1},{4,6},{5,7},{6,4},{7,5},{8,10},{9,11},{10,... | collective-permute-start | bytes 774152 | tf_op jit(solution)/shard_map/ppermute | solution.py:1152
  296.4 21.3 %collective-permute-start.30 = (bf16[336,384]{1,0:T(8,128)(2,1)}, bf16[336,384]{1,0:T(8,128)(2,1)S(1)}, u32[]{:S(2)}, u32[]{:S(2)}) collective-permute-start(bf16[336,384]{1,0:T(8,128)(2,1)} %get-tuple-element.246), channel_id=1, source_target_pairs={{0,4},{1,5},{2,6},{3,7},{4,0},{5,1},{6,2},{7,3},{8,12},{9,13},{10,... | collective-permute-start | bytes 774152 | tf_op jit(solution)/shard_map/ppermute | solution.py:1152
  298.8 19.0 %collective-permute-start.31 = (bf16[336,384]{1,0:T(8,128)(2,1)}, bf16[336,384]{1,0:T(8,128)(2,1)S(1)}, u32[]{:S(2)}, u32[]{:S(2)}) collective-permute-start(bf16[336,384]{1,0:T(8,128)(2,1)} %get-tuple-element.247), channel_id=1, source_target_pairs={{0,6},{1,7},{2,4},{3,5},{4,2},{5,3},{6,0},{7,1},{8,14},{9,15},{10,... | collective-permute-start | bytes 774152 | tf_op jit(solution)/shard_map/ppermute | solution.py:1152
  321.8 14.2 %all-to-all-start.4 = ((f32[32,1,896]{2,1,0:T(1,128)}), f32[32,1,896]{2,1,0:T(1,128)S(1)}, u32[]{:S(2)}, u32[]{:S(2)}) async-start(f32[32,1,896]{2,1,0:T(1,128)} %get-tuple-element.256), calls=%async_computation.4 | async-start | bytes 229376 | tf_op jit(solution)/shard_map/all_to_all | solution.py:1409
  (44 other events, 301.4 us)
